TPU v7x, 512 devices: a whole 4x4x16 slice. The times are simulated.
512 devices in a mesh: kz: 64 (over z, y_lo, core), en: 8 (over y_hi, x).
Axes of the slice: x: 4, y: 4 (y_hi: 2, y_lo: 2; y = y_hi * 2 + y_lo), z: 16, core: 2. Of those that a mesh axis runs over, the one named last changes fastest.
Arguments:
- lesser: bfloat16 [64, 16, 1, 256, 512], P('kz', 'en'), may hold values from -6 to 6
- greater: bfloat16 [64, 16, 1, 256, 512], P('kz', 'en'), may hold values from -6 to 6
- coupling: bfloat16 [1, 4, 256, 256], replicated, may hold values from -0.375 to 0.375
- occupation: float32 [4], replicated, may hold values from 0.2 to 3
- offsets: int32 [4], replicated, may hold values from 1 to 2, as said below
- readers: int32 [64, 5], P('kz'), may hold values 0 or 1
- weights: float32 [5], replicated, may hold values from 0.3 to 1
Outputs:
- sigma_lesser: bfloat16 [64, 16, 1, 256, 512], P('kz', 'en')
- sigma_greater: bfloat16 [64, 16, 1, 256, 512], P('kz', 'en')
Inputs may be any that keep to these rules, and one draw needn't show every extreme that they name: `offsets`: each branch's phonon energy lies between 1 and 2 grid steps, and some branch has exactly 2.
All inputs are finite; a program needn't handle non-finite values. No bound on the sum of `readers` on one device may be relied on, other than what follows from the above.
Results may differ from a plain program's by a relative error of at most 0.018.
Values may be sent and summed in bfloat16 or wider, within the bound.
No kernel may reach another device: no remote copies, remote signals or barrier semaphores. Data moves between devices by JAX's collectives and lax.ppermute only.
A program may use at most 64 MiB of HBM per device.

v0:
```python
import jax
import jax.numpy as jnp
from jax import lax
from jax.sharding import PartitionSpec as P

BRANCHES = 4
REACH = 2
OMAX = 2


def shifted(block, axis, distance):
    devices = range(lax.axis_size(axis))
    route = [((i - distance) % len(devices), i) for i in devices]
    return lax.ppermute(block, axis, route)


def with_halo(value, sides, width):
    for axis, dim in sides:
        count, length = (lax.axis_size(axis), value.shape[dim])
        up = [(i, (i + 1) % count) for i in range(count - 1)]
        down = [(j, i) for i, j in up]
        last = lax.slice_in_dim(value, length - width, length, axis=dim)
        leading = lax.slice_in_dim(value, 0, width, axis=dim)
        before = lax.ppermute(last, axis, up)
        after = lax.ppermute(leading, axis, down)
        value = jnp.concatenate([before, value, after], axis=dim)
    return value


def momentum_window(blocks, factors):
    acc = factors[REACH] * blocks.astype(jnp.float32)
    for distance in range(1, REACH + 1):
        for moved in (distance, -distance):
            piece = shifted(blocks, "kz", moved)
            acc = acc + factors[REACH + moved] * piece.astype(jnp.float32)
    return acc.astype(jnp.bfloat16)


def local(lesser, greater, coupling, occupation, offsets, readers, weights):
    factors = weights * readers[0].astype(jnp.float32)
    stacked = jnp.stack((lesser, greater))
    energies = lesser.shape[1]
    slabs = lesser.shape[2]
    orbitals = lesser.shape[3]
    extended = with_halo(stacked, (("en", 2),), OMAX)
    summed = momentum_window(extended, factors)
    summed = summed.astype(jnp.float32)
    lead = summed.shape[:2]
    total = jnp.zeros(lead + (energies, slabs, orbitals, 2, orbitals), jnp.float32)
    for branch in range(BRANCHES):
        shift = offsets[branch]
        occ = occupation[branch]
        upper = lax.dynamic_slice_in_dim(summed, OMAX + shift, energies, 2)
        lower = lax.dynamic_slice_in_dim(summed, OMAX - shift, energies, 2)
        mixed_l = (occ + 1.0) * upper[0] + occ * lower[0]
        mixed_g = occ * upper[1] + (occ + 1.0) * lower[1]
        mixed = jnp.stack((mixed_l, mixed_g)).astype(jnp.bfloat16)
        matrix = coupling[:, branch]
        left = jnp.einsum("sij,akesjc->akesic", matrix, mixed, preferred_element_type=jnp.float32)
        left = left.astype(jnp.bfloat16).reshape(lead + (energies, slabs, orbitals, 2, orbitals))
        total = total + jnp.einsum(
            "akesirc,sjc->akesirj", left, matrix, preferred_element_type=jnp.float32
        )
    result = total.reshape(lead + (energies, slabs, orbitals, 2 * orbitals)).astype(jnp.bfloat16)
    return (result[0], result[1])


def solution(mesh):
    return jax.shard_map(
        local,
        mesh=mesh,
        in_specs=(
            P("kz", "en", None, None, None),
            P("kz", "en", None, None, None),
            P(),
            P(),
            P(),
            P("kz", None),
            P(),
        ),
        out_specs=(P("kz", "en", None, None, None), P("kz", "en", None, None, None)),
        check_vma=False,
    )
```

profile of v0, /device:TPU:6, one launch (start us, length us, event | category | flops | bytes accessed | tf_op | source)
XLA Modules:
  0.0 269.9 jit_solution(4810823566631669301)
XLA Ops:
  0.6 1.2 copy.9
  1.9 1.2 copy.10
  3.1 0.1 pad_maximum_fusion.1
  3.2 0.0 copy-start.1
  3.2 0.0 copy-start.2
  3.3 0.0 copy-start.3
  3.3 0.0 copy-start.4
  3.3 5.1 %collective-permute-start = (bf16[2,1,2,1,256,512]{4,5,2,3,1,0:T(8,128)(2,1)S(1)}, bf16[2,1,2,1,256,512]{4,5,2,3,1,0:T(8,128)(2,1)S(1)}, u32[]{:S(2)}, u32[]{:S(2)}) collective-permute-start(bf16[2,1,2,1,256,512]{4,5,2,3,1,0:T(8,128)(2,1)S(1)} %pad_maximum_fusion.1), channel_id=1, source_target_pairs={{0,1},{1,2},{2,3},{3,4},{4,5},{5,6},{6,7},{8,9},{9,10},{10,11},{11... | collective-permute-start | bytes 3145736 | tf_op jit(solution)/shard_map/ppermute | solution.py:24
  8.4 1.9 collective-permute-start.1
  10.4 20.5 %collective-permute-done = bf16[2,1,2,1,256,512]{4,5,2,3,1,0:T(8,128)(2,1)S(1)} collective-permute-done((bf16[2,1,2,1,256,512]{4,5,2,3,1,0:T(8,128)(2,1)S(1)}, bf16[2,1,2,1,256,512]{4,5,2,3,1,0:T(8,128)(2,1)S(1)}, u32[]{:S(2)}, u32[]{:S(2)}) %collective-permute-start) | collective-permute-done | bytes 1048608 | tf_op jit(solution)/shard_map/ppermute | solution.py:24
  30.8 7.7 %collective-permute-done.1 = bf16[2,1,2,1,256,512]{4,5,2,3,1,0:T(8,128)(2,1)S(1)} collective-permute-done((bf16[2,1,2,1,256,512]{4,5,2,3,1,0:T(8,128)(2,1)S(1)}, bf16[2,1,2,1,256,512]{4,5,2,3,1,0:T(8,128)(2,1)S(1)}, u32[]{:S(2)}, u32[]{:S(2)}) %collective-permute-start.1) | collective-permute-done | bytes 1048608 | tf_op jit(solution)/shard_map/ppermute | solution.py:25
  38.6 1.8 pad_maximum_fusion
  40.4 1.9 collective-permute-start.2
  42.3 9.8 %collective-permute-start.3 = (bf16[2,1,6,1,256,512]{4,5,2,3,1,0:T(8,128)(2,1)}, bf16[2,1,6,1,256,512]{4,5,2,3,1,0:T(8,128)(2,1)}, u32[]{:S(2)}, u32[]{:S(2)}) collective-permute-start(bf16[2,1,6,1,256,512]{4,5,2,3,1,0:T(8,128)(2,1)} %pad_maximum_fusion), channel_id=1, source_target_pairs={{8,0},{16,8},{24,16},{32,24},{40,32},{48,40},{56,48},{64,56},{72,6... | collective-permute-start | bytes 9437192 | tf_op jit(solution)/shard_map/ppermute | solution.py:14
  52.1 1.9 collective-permute-start.4
  54.0 6.0 %collective-permute-start.5 = (bf16[2,1,6,1,256,512]{4,5,2,3,1,0:T(8,128)(2,1)}, bf16[2,1,6,1,256,512]{4,5,2,3,1,0:T(8,128)(2,1)}, u32[]{:S(2)}, u32[]{:S(2)}) collective-permute-start(bf16[2,1,6,1,256,512]{4,5,2,3,1,0:T(8,128)(2,1)} %pad_maximum_fusion), channel_id=1, source_target_pairs={{16,0},{24,8},{32,16},{40,24},{48,32},{56,40},{64,48},{72,56},{80,... | collective-permute-start | bytes 9437192 | tf_op jit(solution)/shard_map/ppermute | solution.py:14
  60.0 0.0 copy-done.1
  60.0 0.6 fusion.63
  70.6 0.0 copy-done.2
  70.6 0.7 fusion.62
  73.8 0.0 copy-done.3
  73.8 0.0 copy-done.4
  73.8 0.7 fusion.64
  74.5 36.4 %collective-permute-done.2 = bf16[2,1,6,1,256,512]{4,5,2,3,1,0:T(8,128)(2,1)} collective-permute-done((bf16[2,1,6,1,256,512]{4,5,2,3,1,0:T(8,128)(2,1)}, bf16[2,1,6,1,256,512]{4,5,2,3,1,0:T(8,128)(2,1)}, u32[]{:S(2)}, u32[]{:S(2)}) %collective-permute-start.2) | collective-permute-done | bytes 3145760 | tf_op jit(solution)/shard_map/ppermute | solution.py:14
  110.9 4.8 %collective-permute-done.3 = bf16[2,1,6,1,256,512]{4,5,2,3,1,0:T(8,128)(2,1)} collective-permute-done((bf16[2,1,6,1,256,512]{4,5,2,3,1,0:T(8,128)(2,1)}, bf16[2,1,6,1,256,512]{4,5,2,3,1,0:T(8,128)(2,1)}, u32[]{:S(2)}, u32[]{:S(2)}) %collective-permute-start.3) | collective-permute-done | bytes 3145760 | tf_op jit(solution)/shard_map/ppermute | solution.py:14
  115.7 102.5 %collective-permute-done.4 = bf16[2,1,6,1,256,512]{4,5,2,3,1,0:T(8,128)(2,1)} collective-permute-done((bf16[2,1,6,1,256,512]{4,5,2,3,1,0:T(8,128)(2,1)}, bf16[2,1,6,1,256,512]{4,5,2,3,1,0:T(8,128)(2,1)}, u32[]{:S(2)}, u32[]{:S(2)}) %collective-permute-start.4) | collective-permute-done | bytes 3145760 | tf_op jit(solution)/shard_map/ppermute | solution.py:14
  218.3 32.4 %collective-permute-done.5 = bf16[2,1,6,1,256,512]{4,5,2,3,1,0:T(8,128)(2,1)} collective-permute-done((bf16[2,1,6,1,256,512]{4,5,2,3,1,0:T(8,128)(2,1)}, bf16[2,1,6,1,256,512]{4,5,2,3,1,0:T(8,128)(2,1)}, u32[]{:S(2)}, u32[]{:S(2)}) %collective-permute-start.5) | collective-permute-done | bytes 3145760 | tf_op jit(solution)/shard_map/ppermute | solution.py:14
  250.7 9.4 %fusion = f32[2,1,6,1,256,512]{4,5,2,3,1,0:T(8,128)S(1)} fusion(bf16[2,1,6,1,256,512]{4,5,2,3,1,0:T(8,128)(2,1)} %collective-permute-done.5, bf16[2,1,6,1,256,512]{4,5,2,3,1,0:T(8,128)(2,1)} %collective-permute-done.4, bf16[2,1,6,1,256,512]{4,5,2,3,1,0:T(8,128)(2,1)} %collective-permute-done.3, bf16[2,1,6,1,256,512]{4,5,2,3,1,0:T(8,128)(2,1)} %collective-permute-done.2, ...), kind=kLoop, calls=%fused_computation.1 | loop fusion | flops 29884416 | bytes 22020116 | tf_op jit(solution)/shard_map/convert_element_type | solution.py:47
  260.1 0.0 copy-start
  260.1 3.9 %fusion.32 = (bf16[1,2,256,512]{2,3,1,0:T(8,128)(2,1)S(1)}, bf16[1,2,256,512]{2,3,1,0:T(8,128)(2,1)S(1)}, bf16[1,2,256,512]{2,3,1,0:T(8,128)(2,1)S(1)}, bf16[1,2...) fusion(f32[2,1,6,1,256,512]{4,5,2,3,1,0:T(8,128)S(1)} %fusion, ...), kind=kLoop, calls=%fused_computation.56 | loop fusion | flops 8388608 | bytes 20971588 | tf_op jit(solution)/shard_map/stack | solution.py:57
  264.0 0.0 copy-done
  264.1 0.5 convolution_convert_fusion.2
  264.5 0.4 fusion.43
  265.0 0.5 convolution_convert_fusion.3
  265.4 0.4 fusion.46
  265.9 0.5 convolution_convert_fusion.1
  266.4 0.4 fusion.40
  266.8 0.5 convolution_convert_fusion
  267.3 0.5 fusion.1
  267.8 0.1 fusion.61
  267.9 1.0 copy.15
  268.9 1.0 copy.16
  (1 shorter events, 0.0 us)
Async XLA Ops:
  3.2 56.8 %copy-start.1 = (s32[4]{0:T(128)S(1)}, s32[4]{0:T(128)}, u32[]{:S(2)}) copy-start(s32[4]{0:T(128)} %param.11) | copy-start | bytes 52
  3.2 67.4 %copy-start.2 = (f32[4]{0:T(128)S(1)}, f32[4]{0:T(128)}, u32[]{:S(2)}) copy-start(f32[4]{0:T(128)} %param.10) | copy-start | bytes 52
  3.3 70.5 %copy-start.3 = (f32[5]{0:T(128)S(1)}, f32[5]{0:T(128)}, u32[]{:S(2)}) copy-start(f32[5]{0:T(128)} %param.13) | copy-start | bytes 64
  3.3 70.5 %copy-start.4 = (s32[1,5]{1,0:T(1,128)S(1)}, s32[1,5]{1,0:T(1,128)}, u32[]{:S(2)}) copy-start(s32[1,5]{1,0:T(1,128)} %param.12) | copy-start | bytes 64
  3.3 27.6 %collective-permute-start = (bf16[2,1,2,1,256,512]{4,5,2,3,1,0:T(8,128)(2,1)S(1)}, bf16[2,1,2,1,256,512]{4,5,2,3,1,0:T(8,128)(2,1)S(1)}, u32[]{:S(2)}, u32[]{:S(2)}) collective-permute-start(bf16[2,1,2,1,256,512]{4,5,2,3,1,0:T(8,128)(2,1)S(1)} %pad_maximum_fusion.1), channel_id=1, source_target_pairs={{0,1},{1,2},{2,3},{3,4},{4,5},{5,6},{6,7},{8,9},{9,10},{10,11},{11... | collective-permute-start | bytes 3145736 | tf_op jit(solution)/shard_map/ppermute | solution.py:24
  8.4 30.1 %collective-permute-start.1 = (bf16[2,1,2,1,256,512]{4,5,2,3,1,0:T(8,128)(2,1)S(1)}, bf16[2,1,2,1,256,512]{4,5,2,3,1,0:T(8,128)(2,1)S(1)}, u32[]{:S(2)}, u32[]{:S(2)}) collective-permute-start(bf16[2,1,2,1,256,512]{4,5,2,3,1,0:T(8,128)(2,1)S(1)} %pad_maximum_fusion.1), channel_id=1, source_target_pairs={{1,0},{2,1},{3,2},{4,3},{5,4},{6,5},{7,6},{9,8},{10,9},{11,10},{12... | collective-permute-start | bytes 3145736 | tf_op jit(solution)/shard_map/ppermute | solution.py:25
  40.4 70.5 %collective-permute-start.2 = (bf16[2,1,6,1,256,512]{4,5,2,3,1,0:T(8,128)(2,1)}, bf16[2,1,6,1,256,512]{4,5,2,3,1,0:T(8,128)(2,1)}, u32[]{:S(2)}, u32[]{:S(2)}) collective-permute-start(bf16[2,1,6,1,256,512]{4,5,2,3,1,0:T(8,128)(2,1)} %pad_maximum_fusion), channel_id=1, source_target_pairs={{504,0},{0,8},{8,16},{16,24},{24,32},{32,40},{40,48},{48,56},{56,6... | collective-permute-start | bytes 9437192 | tf_op jit(solution)/shard_map/ppermute | solution.py:14
  42.3 73.4 %collective-permute-start.3 = (bf16[2,1,6,1,256,512]{4,5,2,3,1,0:T(8,128)(2,1)}, bf16[2,1,6,1,256,512]{4,5,2,3,1,0:T(8,128)(2,1)}, u32[]{:S(2)}, u32[]{:S(2)}) collective-permute-start(bf16[2,1,6,1,256,512]{4,5,2,3,1,0:T(8,128)(2,1)} %pad_maximum_fusion), channel_id=1, source_target_pairs={{8,0},{16,8},{24,16},{32,24},{40,32},{48,40},{56,48},{64,56},{72,6... | collective-permute-start | bytes 9437192 | tf_op jit(solution)/shard_map/ppermute | solution.py:14
  52.1 166.2 %collective-permute-start.4 = (bf16[2,1,6,1,256,512]{4,5,2,3,1,0:T(8,128)(2,1)}, bf16[2,1,6,1,256,512]{4,5,2,3,1,0:T(8,128)(2,1)}, u32[]{:S(2)}, u32[]{:S(2)}) collective-permute-start(bf16[2,1,6,1,256,512]{4,5,2,3,1,0:T(8,128)(2,1)} %pad_maximum_fusion), channel_id=1, source_target_pairs={{496,0},{504,8},{0,16},{8,24},{16,32},{24,40},{32,48},{40,56},{48,... | collective-permute-start | bytes 9437192 | tf_op jit(solution)/shard_map/ppermute | solution.py:14
  54.0 196.7 %collective-permute-start.5 = (bf16[2,1,6,1,256,512]{4,5,2,3,1,0:T(8,128)(2,1)}, bf16[2,1,6,1,256,512]{4,5,2,3,1,0:T(8,128)(2,1)}, u32[]{:S(2)}, u32[]{:S(2)}) collective-permute-start(bf16[2,1,6,1,256,512]{4,5,2,3,1,0:T(8,128)(2,1)} %pad_maximum_fusion), channel_id=1, source_target_pairs={{16,0},{24,8},{32,16},{40,24},{48,32},{56,40},{64,48},{72,56},{80,... | collective-permute-start | bytes 9437192 | tf_op jit(solution)/shard_map/ppermute | solution.py:14
  260.1 4.0 %copy-start = (bf16[1,4,256,256]{3,2,1,0:T(8,128)(2,1)S(1)}, bf16[1,4,256,256]{3,2,1,0:T(8,128)(2,1)}, u32[]{:S(2)}) copy-start(bf16[1,4,256,256]{3,2,1,0:T(8,128)(2,1)} %param.9) | copy-start | bytes 1572868
where the time goes:
time: 270 us
  waiting for transfers between devices  204 us (76%)
  starting transfers between devices  26.7 us (10%)
  other arithmetic  15.2 us (6%)
  between operations  13.3 us (5%)
  local copies, waits for them, and re-layouts  6.53 us (2%)
  matrix products  3.71 us (1%)
    ppermute x4, waiting for transfers between devices, shifted(): return lax.ppermute(block, axis, route)  176 us
    ppermute x1, waiting for transfers between devices, with_halo(): before = lax.ppermute(last, axis, up)  20.5 us
    ppermute x4, starting transfers between devices, shifted(): return lax.ppermute(block, axis, route)  19.6 us
    convert_element_type x1, other arithmetic, local(): summed = summed.astype(jnp.float32)  9.4 us
    ppermute x1, waiting for transfers between devices, with_halo(): after = lax.ppermute(leading, axis, down)  7.73 us
  transfers between devices with their start and end apart: 6, of which 6 were waited for; matrix products, arithmetic and copies ran while one was open for 1% of the time, Pallas kernels for 0%

commit v1 on v0

v1 whole, which is shorter than its diff:
```python
import jax
import jax.numpy as jnp
from jax import lax
from jax.experimental import pallas as pl
from jax.experimental.pallas import tpu as pltpu
from jax.sharding import PartitionSpec as P

BRANCHES = 4
ORB = 256
F32 = jnp.float32
BF16 = jnp.bfloat16


def swap_route(count, bit):
    return [(k, k ^ bit) for k in range(count)]


def plane_route(count, sign):
    return [(k, (k + (sign if (k >> 1) % 2 == 0 else -sign) * 4) % count) for k in range(count)]


def mix(terms):
    acc = terms[0][0] * terms[0][1].astype(F32)
    for factor, block in terms[1:]:
        acc = acc + factor * block.astype(F32)
    return acc.astype(BF16)


def sigma_kernel(occ_ref, off_ref, own_ref, above_ref, below_ref, mat_ref, tra_ref, out_ref, acc_ref, *, plus_up):
    for branch in range(BRANCHES):
        n = occ_ref[branch]
        one = off_ref[branch] == 1
        up_factor = n + 1.0 if plus_up else n
        down_factor = n if plus_up else n + 1.0
        c = mat_ref[branch]
        t = tra_ref[branch]
        for e in range(2):
            if e == 0:
                upper = jnp.where(one, own_ref[1], above_ref[0])
                lower = jnp.where(one, below_ref[1], below_ref[0])
            else:
                upper = jnp.where(one, above_ref[0], above_ref[1])
                lower = jnp.where(one, own_ref[0], below_ref[1])
            mixed = (up_factor * upper.astype(F32) + down_factor * lower.astype(F32)).astype(BF16)
            left = jnp.dot(c, mixed, preferred_element_type=F32).astype(BF16)
            for h in range(2):
                cols = slice(h * ORB, (h + 1) * ORB)
                right = jnp.dot(left[:, cols], t, preferred_element_type=F32)
                if branch == 0:
                    acc_ref[e, :, cols] = right
                elif branch < BRANCHES - 1:
                    acc_ref[e, :, cols] += right
                else:
                    out_ref[e, :, cols] = (acc_ref[e, :, cols] + right).astype(BF16)


def sigma(own, above, below, mats, trans, occupation, offsets, plus_up):
    import functools

    vmem = pl.BlockSpec(memory_space=pltpu.VMEM)
    smem = pl.BlockSpec(memory_space=pltpu.SMEM)
    return pl.pallas_call(
        functools.partial(sigma_kernel, plus_up=plus_up),
        out_shape=jax.ShapeDtypeStruct(own.shape, BF16),
        in_specs=[smem, smem, vmem, vmem, vmem, vmem, vmem],
        out_specs=vmem,
        scratch_shapes=[pltpu.VMEM(own.shape, F32)],
        compiler_params=pltpu.CompilerParams(vmem_limit_bytes=24 * 1024 * 1024),
        cost_estimate=pl.CostEstimate(flops=2**30, bytes_accessed=3 * 2**20, transcendentals=0),
    )(occupation, offsets, own, above, below, mats, trans)


def local(lesser, greater, coupling, occupation, offsets, readers, weights):
    count = lax.axis_size("kz")
    energies = lax.axis_size("en")
    k = lax.axis_index("kz")
    core1 = (k & 1) == 1
    odd = ((k >> 1) & 1) == 1
    up = [(i, i + 1) for i in range(energies - 1)]
    down = [(i + 1, i) for i in range(energies - 1)]

    def kz(block, route):
        return lax.ppermute(block, "kz", route)

    shape = (2, ORB, 2 * ORB)
    xl = lesser.reshape(shape)
    xg = greater.reshape(shape)
    mats = coupling[0]
    trans = jnp.swapaxes(mats, 1, 2)
    f = weights * readers[0].astype(F32)
    fc = kz(f, swap_route(count, 1))
    fy = kz(f, swap_route(count, 2))

    yl = kz(xl, swap_route(count, 2))
    zg = kz(xg, plane_route(count, -1))
    cg = kz(xg, swap_route(count, 1))
    zl = kz(yl, plane_route(count, 1))
    czg = kz(zg, swap_route(count, 1))
    zero = jnp.zeros((), F32)
    pg = mix([
        (jnp.where(odd, fy[0], fy[4]), xg),
        (jnp.where(odd, fy[4], fy[0]), zg),
        (jnp.where(odd, jnp.where(core1, fy[1], zero), jnp.where(core1, zero, fy[3])), cg),
        (jnp.where(odd, jnp.where(core1, zero, fy[3]), jnp.where(core1, fy[1], zero)), czg),
    ])
    rg = kz(pg, swap_route(count, 2))
    wg = mix([(f[2], xg), (jnp.where(core1, f[3], f[1]), cg), (jnp.ones((), F32), rg)])
    far = jnp.where(core1, fc[3], fc[1])
    ql = mix([
        (jnp.where(core1, fc[1], fc[3]), xl),
        (jnp.where(odd == core1, far, zero), yl),
        (jnp.where(odd == core1, zero, far), zl),
    ])
    rl = kz(ql, swap_route(count, 1))
    wl = mix([
        (f[2], xl),
        (jnp.where(odd, f[4], f[0]), yl),
        (jnp.where(odd, f[0], f[4]), zl),
        (jnp.ones((), F32), rl),
    ])

    def en(block):
        below = lax.ppermute(block, "en", up)
        above = lax.ppermute(block, "en", down)
        return above, below

    al, bl = en(wl)
    ag, bg = en(wg)
    sl = sigma(wl, al, bl, mats, trans, occupation, offsets, True)
    sg = sigma(wg, ag, bg, mats, trans, occupation, offsets, False)
    return sl.reshape(lesser.shape), sg.reshape(greater.shape)


def solution(mesh):
    wide = P("kz", "en", None, None, None)
    return jax.shard_map(
        local,
        mesh=mesh,
        in_specs=(wide, wide, P(), P(), P(), P("kz", None), P()),
        out_specs=(wide, wide),
        check_vma=False,
    )
```

time: 270 us -> 102 us (0.38)
  waiting for transfers between devices: 204 us -> 18.5 us
  starting transfers between devices: 26.7 us -> 53.2 us
  Pallas kernels: 0 us -> 7.29 us
  other arithmetic: 15.2 us -> 8.67 us
  local copies, waits for them, and re-layouts: 6.53 us -> 2.81 us
  matrix products: 3.71 us -> 0 us
    ppermute x6 -> x13, waiting for transfers between devices: 204 us -> 18.5 us  [the longest x2 13 us: en(): above = lax.ppermute(block, 'en', down)]
    ppermute x6 -> x13, starting transfers between devices: 26.7 us -> 53.2 us  [the longest x9 37 us: kz(): return lax.ppermute(block, 'kz', route)]
    pallas_call x0 -> x2, Pallas kernels: none -> 7.29 us  [sigma(): pl.pallas_call(functools.partial(sigma_kernel, plus_up=plus_up), out_shap...]
    another operation x2 -> x0, other arithmetic: 4.03 us -> none  [the longest x1 3.93 us: local(): mixed = jnp.stack((mixed_l, mixed_g)).astype(jnp.bfloat16)]
    dot_general x8 -> x0, matrix products: 3.71 us -> none  [the longest x4 1.91 us: local(): jnp.einsum('sij,akesjc->akesic', matrix, mixed, preferred_element_type=jn...]
    unnamed x14 -> x19, local copies, waits for them, and re-layouts: 4.53 us -> 0.91 us
    convert_element_type x1 -> x4, other arithmetic: 9.4 us -> 8.66 us  [mix(): return acc.astype(BF16)]
  transfers between devices with their start and end apart: 6 -> 13, of which waited for: 6 -> 4; matrix products, arithmetic and copies ran while one was open for 1% -> 11% of each run, Pallas kernels for 0% -> 3%
where the time goes in v1:
time: 102 us
  starting transfers between devices  53.2 us (52%)
  waiting for transfers between devices  18.5 us (18%)
  between operations  11.1 us (11%)
  other arithmetic  8.67 us (8%)
  Pallas kernels  7.29 us (7%)
  local copies, waits for them, and re-layouts  2.81 us (3%)
    ppermute x9, starting transfers between devices, kz(): return lax.ppermute(block, 'kz', route)  37 us
    ppermute x2, waiting for transfers between devices, en(): above = lax.ppermute(block, 'en', down)  13 us
    ppermute x2, starting transfers between devices, en(): below = lax.ppermute(block, 'en', up)  12.4 us
    convert_element_type x4, other arithmetic, mix(): return acc.astype(BF16)  8.66 us
    pallas_call x2, Pallas kernels, sigma(): pl.pallas_call(functools.partial(sigma_kernel, plus_up=plus_up), out_shap...  7.29 us
    ppermute x9, waiting for transfers between devices, kz(): return lax.ppermute(block, 'kz', route)  5.46 us
    ppermute x2, starting transfers between devices, en(): above = lax.ppermute(block, 'en', down)  3.84 us
  transfers between devices with their start and end apart: 13, of which 4 were waited for; matrix products, arithmetic and copies ran while one was open for 11% of the time, Pallas kernels for 3%

profile of v1, /device:TPU:6, one launch (start us, length us, event | category | flops | bytes accessed | tf_op | source)
XLA Modules:
  0.0 101.6 jit_solution(11140185337393090256)
XLA Ops:
  0.6 0.0 copy-start.7
  0.6 0.0 copy-start.8
  0.6 3.6 %collective-permute-start = (bf16[2,256,512]{2,1,0:T(8,128)(2,1)}, bf16[2,256,512]{2,1,0:T(8,128)(2,1)S(1)}, u32[]{:S(2)}, u32[]{:S(2)}) collective-permute-start(bf16[2,256,512]{2,1,0:T(8,128)(2,1)} %bitcast.33), channel_id=1, source_target_pairs={{0,16},{8,24},{16,0},{24,8},{32,48},{40,56},{48,32},{56,40},{64,80... | collective-permute-start | bytes 1572872 | tf_op jit(solution)/shard_map/ppermute | solution.py:83
  4.3 11.4 %collective-permute-start.8 = (bf16[2,256,512]{2,1,0:T(8,128)(2,1)}, bf16[2,256,512]{2,1,0:T(8,128)(2,1)S(1)}, u32[]{:S(2)}, u32[]{:S(2)}) collective-permute-start(bf16[2,256,512]{2,1,0:T(8,128)(2,1)} %bitcast.34), channel_id=1, source_target_pairs={{0,480},{8,488},{16,48},{24,56},{32,0},{40,8},{48,80},{56,88},{64,... | collective-permute-start | bytes 1572872 | tf_op jit(solution)/shard_map/ppermute | solution.py:83
  15.7 0.9 collective-permute-done
  16.6 3.8 %collective-permute-start.1 = (bf16[2,256,512]{2,1,0:T(8,128)(2,1)S(1)}, bf16[2,256,512]{2,1,0:T(8,128)(2,1)S(1)}, u32[]{:S(2)}, u32[]{:S(2)}) collective-permute-start(bf16[2,256,512]{2,1,0:T(8,128)(2,1)S(1)} %collective-permute-done), channel_id=1, source_target_pairs={{0,32},{8,40},{16,496},{24,504},{32,64},{40,72},{48,16},{56,24},{6... | collective-permute-start | bytes 1572872 | tf_op jit(solution)/shard_map/ppermute | solution.py:83
  20.4 1.9 %collective-permute-start.6 = (bf16[2,256,512]{2,1,0:T(8,128)(2,1)}, bf16[2,256,512]{2,1,0:T(8,128)(2,1)S(1)}, u32[]{:S(2)}, u32[]{:S(2)}) collective-permute-start(bf16[2,256,512]{2,1,0:T(8,128)(2,1)} %bitcast.35), channel_id=1, source_target_pairs={{0,8},{8,0},{16,24},{24,16},{32,40},{40,32},{48,56},{56,48},{64,72... | collective-permute-start | bytes 1572872 | tf_op jit(solution)/shard_map/ppermute | solution.py:83
  22.3 4.6 %collective-permute-done.8 = bf16[2,256,512]{2,1,0:T(8,128)(2,1)S(1)} collective-permute-done((bf16[2,256,512]{2,1,0:T(8,128)(2,1)}, bf16[2,256,512]{2,1,0:T(8,128)(2,1)S(1)}, u32[]{:S(2)}, u32[]{:S(2)}) %collective-permute-start.8) | collective-permute-done | bytes 524320 | tf_op jit(solution)/shard_map/ppermute | solution.py:83
  26.9 1.9 %collective-permute-start.9 = (bf16[2,256,512]{2,1,0:T(8,128)(2,1)S(1)}, bf16[2,256,512]{2,1,0:T(8,128)(2,1)}, u32[]{:S(2)}, u32[]{:S(2)}) collective-permute-start(bf16[2,256,512]{2,1,0:T(8,128)(2,1)S(1)} %collective-permute-done.8), channel_id=1, source_target_pairs={{0,8},{8,0},{16,24},{24,16},{32,40},{40,32},{48,56},{56,48},{64,72... | collective-permute-start | bytes 1572872 | tf_op jit(solution)/shard_map/ppermute | solution.py:83
  28.8 0.0 copy-done.7
  28.8 0.0 copy-done.8
  28.8 7.0 %collective-permute-start.7 = (f32[5]{0:T(128)S(1)}, f32[5]{0:T(128)S(1)}, u32[]{:S(2)}, u32[]{:S(2)}) collective-permute-start(f32[5]{0:T(128)S(1)} %bitcast_multiply_fusion), channel_id=1, source_target_pairs={{0,16},{8,24},{16,0},{24,8},{32,48},{40,56},{48,32},{56,40},{64,80... | collective-permute-start | bytes 68 | tf_op jit(solution)/shard_map/ppermute | solution.py:83
  35.8 1.9 %collective-permute-start.2 = (f32[5]{0:T(128)S(1)}, f32[5]{0:T(128)S(1)}, u32[]{:S(2)}, u32[]{:S(2)}) collective-permute-start(f32[5]{0:T(128)S(1)} %bitcast_multiply_fusion), channel_id=1, source_target_pairs={{0,8},{8,0},{16,24},{24,16},{32,40},{40,32},{48,56},{56,48},{64,72... | collective-permute-start | bytes 68 | tf_op jit(solution)/shard_map/ppermute | solution.py:83
  37.8 0.0 collective-permute-done.7
  37.8 0.6 fusion.15
  39.7 0.0 collective-permute-done.2
  39.7 0.6 fusion.16
  42.9 0.0 copy-start.4
  42.9 0.0 collective-permute-done.1
  43.0 2.2 %fusion.6 = bf16[2,256,512]{2,1,0:T(8,128)(2,1)} fusion(bf16[2,256,512]{2,1,0:T(8,128)(2,1)S(1)} %collective-permute-done, bf16[2,256,512]{2,1,0:T(8,128)(2,1)S(1)} %collective-permute-done.1, f32[]{:T(128)S(6)} %select_n.47, f32[]{:T(128)S(6)} %select_n.46, f32[]{:T(128)S(6)} %select_n.44, bf16[1,2,1,256,512]{4,3,2,1,0:T(8,128)(2,1)} %param.7), kind=kLoop, calls=%fused_computation.16 | loop fusion | flops 2359296 | bytes 2097164 | tf_op jit(solution)/shard_map/convert_element_type | solution.py:26
  45.1 2.4 %collective-permute-start.3 = (bf16[2,256,512]{2,1,0:T(8,128)(2,1)}, bf16[2,256,512]{2,1,0:T(8,128)(2,1)}, u32[]{:S(2)}, u32[]{:S(2)}) collective-permute-start(bf16[2,256,512]{2,1,0:T(8,128)(2,1)} %fusion.6), channel_id=1, source_target_pairs={{0,8},{8,0},{16,24},{24,16},{32,40},{40,32},{48,56},{56,48},{64,72... | collective-permute-start | bytes 1572872 | tf_op jit(solution)/shard_map/ppermute | solution.py:83
  50.1 0.0 copy-start.3
  50.1 0.0 collective-permute-done.6
  50.1 0.0 copy-start.5
  50.2 0.0 collective-permute-done.9
  50.2 2.5 %fusion.13 = bf16[2,256,512]{2,1,0:T(8,128)(2,1)} fusion(bf16[2,256,512]{2,1,0:T(8,128)(2,1)S(1)} %collective-permute-done.6, bf16[2,256,512]{2,1,0:T(8,128)(2,1)} %collective-permute-done.9, bf16[2,256,512]{2,1,0:T(8,128)(2,1)S(1)} %collective-permute-done.8, f32[]{:T(128)S(6)} %select_n.54, f32[]{:T(128)S(6)} %select_n.53, f32[]{:T(128)S(6)} %select_n.50, ...), kind=kLoop, calls=%fused_computation.23 | loop fusion | flops 3145728 | bytes 2621456 | tf_op jit(solution)/shard_map/convert_element_type | solution.py:26
  52.7 0.0 copy-done.5
  52.7 3.0 %collective-permute-start.10 = (bf16[2,256,512]{2,1,0:T(8,128)(2,1)}, bf16[2,256,512]{2,1,0:T(8,128)(2,1)}, u32[]{:S(2)}, u32[]{:S(2)}) collective-permute-start(bf16[2,256,512]{2,1,0:T(8,128)(2,1)} %fusion.13), channel_id=1, source_target_pairs={{0,16},{8,24},{16,0},{24,8},{32,48},{40,56},{48,32},{56,40},{64,80... | collective-permute-start | bytes 1572872 | tf_op jit(solution)/shard_map/ppermute | solution.py:83
  55.6 0.7 fusion.14
  60.0 0.0 collective-permute-done.3
  60.0 0.0 copy-start.6
  60.0 2.1 %fusion.3.own_ref = bf16[2,256,512]{2,1,0:T(8,128)(2,1)S(1)} fusion(bf16[2,256,512]{2,1,0:T(8,128)(2,1)S(1)} %collective-permute-done, bf16[2,256,512]{2,1,0:T(8,128)(2,1)S(1)} %collective-permute-done.1, bf16[2,256,512]{2,1,0:T(8,128)(2,1)} %collective-permute-done.3, f32[]{:T(128)S(6)} %select_n.43, f32[]{:T(128)S(6)} %select_n.42, f32[]{:T(128)} %bitcast.1, ...), kind=kLoop, calls=%fused_computation.13 | loop fusion | flops 2883584 | bytes 2621452 | tf_op jit(solution)/shard_map/convert_element_type | solution.py:26
  62.1 0.0 copy-start
  62.1 4.9 %collective-permute-start.5 = (bf16[2,256,512]{2,1,0:T(8,128)(2,1)S(1)}, bf16[2,256,512]{2,1,0:T(8,128)(2,1)S(1)}, u32[]{:S(2)}, u32[]{:S(2)}) collective-permute-start(bf16[2,256,512]{2,1,0:T(8,128)(2,1)S(1)} %fusion.3.own_ref), channel_id=1, source_target_pairs={{0,1},{1,2},{2,3},{3,4},{4,5},{5,6},{6,7},{8,9},{9,10},{10,11},{11... | collective-permute-start | bytes 1572872 | tf_op jit(solution)/shard_map/ppermute | solution.py:123
  67.0 1.9 %collective-permute-start.4 = (bf16[2,256,512]{2,1,0:T(8,128)(2,1)S(1)}, bf16[2,256,512]{2,1,0:T(8,128)(2,1)S(1)}, u32[]{:S(2)}, u32[]{:S(2)}) collective-permute-start(bf16[2,256,512]{2,1,0:T(8,128)(2,1)S(1)} %fusion.3.own_ref), channel_id=1, source_target_pairs={{1,0},{2,1},{3,2},{4,3},{5,4},{6,5},{7,6},{9,8},{10,9},{11,10},{12... | collective-permute-start | bytes 1572872 | tf_op jit(solution)/shard_map/ppermute | solution.py:124
  68.9 0.0 collective-permute-done.10
  68.9 1.9 %fusion.9.own_ref = bf16[2,256,512]{2,1,0:T(8,128)(2,1)S(1)} fusion(bf16[2,256,512]{2,1,0:T(8,128)(2,1)S(1)} %copy-done.6, bf16[2,256,512]{2,1,0:T(8,128)(2,1)} %collective-permute-done.10, f32[]{:T(128)S(6)} %select_n.48, f32[]{:T(128)} %bitcast.1, bf16[1,2,1,256,512]{4,3,2,1,0:T(8,128)(2,1)S(1)} %copy-done.4), kind=kLoop, calls=%fused_computation.19 | loop fusion | flops 2097152 | bytes 2097160 | tf_op jit(solution)/shard_map/convert_element_type | solution.py:26
  70.9 7.5 %collective-permute-start.12 = (bf16[2,256,512]{2,1,0:T(8,128)(2,1)S(1)}, bf16[2,256,512]{2,1,0:T(8,128)(2,1)}, u32[]{:S(2)}, u32[]{:S(2)}) collective-permute-start(bf16[2,256,512]{2,1,0:T(8,128)(2,1)S(1)} %fusion.9.own_ref), channel_id=1, source_target_pairs={{0,1},{1,2},{2,3},{3,4},{4,5},{5,6},{6,7},{8,9},{9,10},{10,11},{11... | collective-permute-start | bytes 1572872 | tf_op jit(solution)/shard_map/ppermute | solution.py:123
  78.4 1.9 %collective-permute-start.11 = (bf16[2,256,512]{2,1,0:T(8,128)(2,1)S(1)}, bf16[2,256,512]{2,1,0:T(8,128)(2,1)}, u32[]{:S(2)}, u32[]{:S(2)}) collective-permute-start(bf16[2,256,512]{2,1,0:T(8,128)(2,1)S(1)} %fusion.9.own_ref), channel_id=1, source_target_pairs={{1,0},{2,1},{3,2},{4,3},{5,4},{6,5},{7,6},{9,8},{10,9},{11,10},{12... | collective-permute-start | bytes 1572872 | tf_op jit(solution)/shard_map/ppermute | solution.py:124
  80.3 0.2 copy.9
  80.5 0.0 collective-permute-done.5.below_ref
  80.6 6.0 %collective-permute-done.4.above_ref = bf16[2,256,512]{2,1,0:T(8,128)(2,1)S(1)} collective-permute-done((bf16[2,256,512]{2,1,0:T(8,128)(2,1)S(1)}, bf16[2,256,512]{2,1,0:T(8,128)(2,1)S(1)}, u32[]{:S(2)}, u32[]{:S(2)}) %collective-permute-start.4) | collective-permute-done | bytes 524320 | tf_op jit(solution)/shard_map/ppermute | solution.py:124
  86.6 0.7 copy-done.1
  87.2 0.0 copy-done.2
  87.2 3.3 %shard_map.86 = bf16[2,256,512]{2,1,0:T(8,128)(2,1)} custom-call(f32[4]{0:T(128)S(1)} %copy-done.1, s32[4]{0:T(128)S(1)} %copy-done.2, bf16[2,256,512]{2,1,0:T(8,128)(2,1)S(1)} %fusion.3.own_ref, bf16[2,256,512]{2,1,0:T(8,128)(2,1)S(1)} %collective-permute-done.4.above_ref, bf16[2,256,512]{2,1,0:T(8,128)(2,1)S(1)} %collective-permute-done.5.below_ref, ...), custom_call_target="tpu_custom_call" | custom-call | flops 1073741824 | bytes 3145728 | tf_op jit(solution)/shard_map/pallas_call | solution.py:62
  90.6 0.0 collective-permute-done.12.below_ref
  90.6 7.0 %collective-permute-done.11.above_ref = bf16[2,256,512]{2,1,0:T(8,128)(2,1)} collective-permute-done((bf16[2,256,512]{2,1,0:T(8,128)(2,1)S(1)}, bf16[2,256,512]{2,1,0:T(8,128)(2,1)}, u32[]{:S(2)}, u32[]{:S(2)}) %collective-permute-start.11) | collective-permute-done | bytes 524320 | tf_op jit(solution)/shard_map/ppermute | solution.py:124
  97.6 4.0 %shard_map.87 = bf16[2,256,512]{2,1,0:T(8,128)(2,1)} custom-call(f32[4]{0:T(128)S(1)} %copy-done.1, s32[4]{0:T(128)S(1)} %copy-done.2, bf16[2,256,512]{2,1,0:T(8,128)(2,1)S(1)} %fusion.9.own_ref, bf16[2,256,512]{2,1,0:T(8,128)(2,1)} %collective-permute-done.11.above_ref, bf16[2,256,512]{2,1,0:T(8,128)(2,1)} %collective-permute-done.12.below_ref, ...), custom_call_target="tpu_custom_call" | custom-call | flops 1073741824 | bytes 3145728 | tf_op jit(solution)/shard_map/pallas_call | solution.py:62
  (7 shorter events, 0.0 us)
Async XLA Ops:
  0.6 28.2 %copy-start.7 = (f32[5]{0:T(128)S(1)}, f32[5]{0:T(128)}, u32[]{:S(2)}) copy-start(f32[5]{0:T(128)} %param.13) | copy-start | bytes 64
  0.6 28.2 %copy-start.8 = (s32[1,5]{1,0:T(1,128)S(1)}, s32[1,5]{1,0:T(1,128)}, u32[]{:S(2)}) copy-start(s32[1,5]{1,0:T(1,128)} %param.12) | copy-start | bytes 64
  0.6 15.9 %collective-permute-start = (bf16[2,256,512]{2,1,0:T(8,128)(2,1)}, bf16[2,256,512]{2,1,0:T(8,128)(2,1)S(1)}, u32[]{:S(2)}, u32[]{:S(2)}) collective-permute-start(bf16[2,256,512]{2,1,0:T(8,128)(2,1)} %bitcast.33), channel_id=1, source_target_pairs={{0,16},{8,24},{16,0},{24,8},{32,48},{40,56},{48,32},{56,40},{64,80... | collective-permute-start | bytes 1572872 | tf_op jit(solution)/shard_map/ppermute | solution.py:83
  4.3 22.6 %collective-permute-start.8 = (bf16[2,256,512]{2,1,0:T(8,128)(2,1)}, bf16[2,256,512]{2,1,0:T(8,128)(2,1)S(1)}, u32[]{:S(2)}, u32[]{:S(2)}) collective-permute-start(bf16[2,256,512]{2,1,0:T(8,128)(2,1)} %bitcast.34), channel_id=1, source_target_pairs={{0,480},{8,488},{16,48},{24,56},{32,0},{40,8},{48,80},{56,88},{64,... | collective-permute-start | bytes 1572872 | tf_op jit(solution)/shard_map/ppermute | solution.py:83
  16.6 26.4 %collective-permute-start.1 = (bf16[2,256,512]{2,1,0:T(8,128)(2,1)S(1)}, bf16[2,256,512]{2,1,0:T(8,128)(2,1)S(1)}, u32[]{:S(2)}, u32[]{:S(2)}) collective-permute-start(bf16[2,256,512]{2,1,0:T(8,128)(2,1)S(1)} %collective-permute-done), channel_id=1, source_target_pairs={{0,32},{8,40},{16,496},{24,504},{32,64},{40,72},{48,16},{56,24},{6... | collective-permute-start | bytes 1572872 | tf_op jit(solution)/shard_map/ppermute | solution.py:83
  20.4 29.8 %collective-permute-start.6 = (bf16[2,256,512]{2,1,0:T(8,128)(2,1)}, bf16[2,256,512]{2,1,0:T(8,128)(2,1)S(1)}, u32[]{:S(2)}, u32[]{:S(2)}) collective-permute-start(bf16[2,256,512]{2,1,0:T(8,128)(2,1)} %bitcast.35), channel_id=1, source_target_pairs={{0,8},{8,0},{16,24},{24,16},{32,40},{40,32},{48,56},{56,48},{64,72... | collective-permute-start | bytes 1572872 | tf_op jit(solution)/shard_map/ppermute | solution.py:83
  26.9 23.3 %collective-permute-start.9 = (bf16[2,256,512]{2,1,0:T(8,128)(2,1)S(1)}, bf16[2,256,512]{2,1,0:T(8,128)(2,1)}, u32[]{:S(2)}, u32[]{:S(2)}) collective-permute-start(bf16[2,256,512]{2,1,0:T(8,128)(2,1)S(1)} %collective-permute-done.8), channel_id=1, source_target_pairs={{0,8},{8,0},{16,24},{24,16},{32,40},{40,32},{48,56},{56,48},{64,72... | collective-permute-start | bytes 1572872 | tf_op jit(solution)/shard_map/ppermute | solution.py:83
  28.8 8.9 %collective-permute-start.7 = (f32[5]{0:T(128)S(1)}, f32[5]{0:T(128)S(1)}, u32[]{:S(2)}, u32[]{:S(2)}) collective-permute-start(f32[5]{0:T(128)S(1)} %bitcast_multiply_fusion), channel_id=1, source_target_pairs={{0,16},{8,24},{16,0},{24,8},{32,48},{40,56},{48,32},{56,40},{64,80... | collective-permute-start | bytes 68 | tf_op jit(solution)/shard_map/ppermute | solution.py:83
  35.8 3.9 %collective-permute-start.2 = (f32[5]{0:T(128)S(1)}, f32[5]{0:T(128)S(1)}, u32[]{:S(2)}, u32[]{:S(2)}) collective-permute-start(f32[5]{0:T(128)S(1)} %bitcast_multiply_fusion), channel_id=1, source_target_pairs={{0,8},{8,0},{16,24},{24,16},{32,40},{40,32},{48,56},{56,48},{64,72... | collective-permute-start | bytes 68 | tf_op jit(solution)/shard_map/ppermute | solution.py:83
  42.9 7.2 %copy-start.4 = (bf16[1,2,1,256,512]{4,3,2,1,0:T(8,128)(2,1)S(1)}, bf16[1,2,1,256,512]{4,3,2,1,0:T(8,128)(2,1)}, u32[]{:S(2)}) copy-start(bf16[1,2,1,256,512]{4,3,2,1,0:T(8,128)(2,1)} %param.8) | copy-start | bytes 1572868
  45.1 14.9 %collective-permute-start.3 = (bf16[2,256,512]{2,1,0:T(8,128)(2,1)}, bf16[2,256,512]{2,1,0:T(8,128)(2,1)}, u32[]{:S(2)}, u32[]{:S(2)}) collective-permute-start(bf16[2,256,512]{2,1,0:T(8,128)(2,1)} %fusion.6), channel_id=1, source_target_pairs={{0,8},{8,0},{16,24},{24,16},{32,40},{40,32},{48,56},{56,48},{64,72... | collective-permute-start | bytes 1572872 | tf_op jit(solution)/shard_map/ppermute | solution.py:83
  50.1 9.9 %copy-start.3 = (bf16[1,2,1,256,512]{4,3,2,1,0:T(8,128)(2,1)S(1)}, bf16[1,2,1,256,512]{4,3,2,1,0:T(8,128)(2,1)}, u32[]{:S(2)}) copy-start(bf16[1,2,1,256,512]{4,3,2,1,0:T(8,128)(2,1)} %param.7) | copy-start | bytes 1572868
  50.1 2.5 %copy-start.5 = (bf16[2,256,512]{2,1,0:T(8,128)(2,1)}, bf16[2,256,512]{2,1,0:T(8,128)(2,1)S(1)}, u32[]{:S(2)}) copy-start(bf16[2,256,512]{2,1,0:T(8,128)(2,1)S(1)} %collective-permute-done.6) | copy-start | bytes 1572868
  52.7 16.2 %collective-permute-start.10 = (bf16[2,256,512]{2,1,0:T(8,128)(2,1)}, bf16[2,256,512]{2,1,0:T(8,128)(2,1)}, u32[]{:S(2)}, u32[]{:S(2)}) collective-permute-start(bf16[2,256,512]{2,1,0:T(8,128)(2,1)} %fusion.13), channel_id=1, source_target_pairs={{0,16},{8,24},{16,0},{24,8},{32,48},{40,56},{48,32},{56,40},{64,80... | collective-permute-start | bytes 1572872 | tf_op jit(solution)/shard_map/ppermute | solution.py:83
  60.0 8.9 %copy-start.6 = (bf16[2,256,512]{2,1,0:T(8,128)(2,1)S(1)}, bf16[2,256,512]{2,1,0:T(8,128)(2,1)}, u32[]{:S(2)}) copy-start(bf16[2,256,512]{2,1,0:T(8,128)(2,1)} %copy-done.5) | copy-start | bytes 1572868
  62.1 18.2 %copy-start = (bf16[1,4,256,256]{3,2,1,0:T(8,128)(2,1)S(1)}, bf16[1,4,256,256]{3,2,1,0:T(8,128)(2,1)}, u32[]{:S(2)}) copy-start(bf16[1,4,256,256]{3,2,1,0:T(8,128)(2,1)} %param.9) | copy-start | bytes 1572868
  62.1 18.4 %collective-permute-start.5 = (bf16[2,256,512]{2,1,0:T(8,128)(2,1)S(1)}, bf16[2,256,512]{2,1,0:T(8,128)(2,1)S(1)}, u32[]{:S(2)}, u32[]{:S(2)}) collective-permute-start(bf16[2,256,512]{2,1,0:T(8,128)(2,1)S(1)} %fusion.3.own_ref), channel_id=1, source_target_pairs={{0,1},{1,2},{2,3},{3,4},{4,5},{5,6},{6,7},{8,9},{9,10},{10,11},{11... | collective-permute-start | bytes 1572872 | tf_op jit(solution)/shard_map/ppermute | solution.py:123
  67.0 19.6 %collective-permute-start.4 = (bf16[2,256,512]{2,1,0:T(8,128)(2,1)S(1)}, bf16[2,256,512]{2,1,0:T(8,128)(2,1)S(1)}, u32[]{:S(2)}, u32[]{:S(2)}) collective-permute-start(bf16[2,256,512]{2,1,0:T(8,128)(2,1)S(1)} %fusion.3.own_ref), channel_id=1, source_target_pairs={{1,0},{2,1},{3,2},{4,3},{5,4},{6,5},{7,6},{9,8},{10,9},{11,10},{12... | collective-permute-start | bytes 1572872 | tf_op jit(solution)/shard_map/ppermute | solution.py:124
  70.9 19.7 %collective-permute-start.12 = (bf16[2,256,512]{2,1,0:T(8,128)(2,1)S(1)}, bf16[2,256,512]{2,1,0:T(8,128)(2,1)}, u32[]{:S(2)}, u32[]{:S(2)}) collective-permute-start(bf16[2,256,512]{2,1,0:T(8,128)(2,1)S(1)} %fusion.9.own_ref), channel_id=1, source_target_pairs={{0,1},{1,2},{2,3},{3,4},{4,5},{5,6},{6,7},{8,9},{9,10},{10,11},{11... | collective-permute-start | bytes 1572872 | tf_op jit(solution)/shard_map/ppermute | solution.py:123
  78.4 19.2 %collective-permute-start.11 = (bf16[2,256,512]{2,1,0:T(8,128)(2,1)S(1)}, bf16[2,256,512]{2,1,0:T(8,128)(2,1)}, u32[]{:S(2)}, u32[]{:S(2)}) collective-permute-start(bf16[2,256,512]{2,1,0:T(8,128)(2,1)S(1)} %fusion.9.own_ref), channel_id=1, source_target_pairs={{1,0},{2,1},{3,2},{4,3},{5,4},{6,5},{7,6},{9,8},{10,9},{11,10},{12... | collective-permute-start | bytes 1572872 | tf_op jit(solution)/shard_map/ppermute | solution.py:124
  86.6 0.7 copy-start.1
  86.6 0.7 copy-start.2

commit v2 on v1

v2 whole, which is shorter than its diff:
```python
import functools

import jax
import jax.numpy as jnp
from jax import lax
from jax.experimental import pallas as pl
from jax.experimental.pallas import tpu as pltpu
from jax.sharding import PartitionSpec as P

BRANCHES = 4
ORB = 256
SHAPE = (2, ORB, 2 * ORB)
ROWS = 32
F32 = jnp.float32
BF16 = jnp.bfloat16
VMEM = pl.BlockSpec(memory_space=pltpu.VMEM)
SMEM = pl.BlockSpec(memory_space=pltpu.SMEM)
PARAMS = pltpu.CompilerParams(vmem_limit_bytes=24 * 1024 * 1024)


def swap_route(count, bit):
    return [(k, k ^ bit) for k in range(count)]


def plane_route(count, sign):
    return [(k, (k + (sign if (k >> 1) % 2 == 0 else -sign) * 4) % count) for k in range(count)]


def pair_route(count, first):
    pairs = [(i, i + 1) for i in range(first, count - 1, 2)]
    return pairs + [(j, i) for i, j in pairs]


def weighted(factors, refs, out_ref):
    for e in range(2):
        for r in range(0, ORB, ROWS):
            rows = slice(r, r + ROWS)
            acc = None
            for factor, ref in zip(factors, refs):
                term = ref[e, rows, :].astype(F32)
                if factor is not None:
                    term = factor * term
                acc = term if acc is None else acc + term
            out_ref[e, rows, :] = acc.astype(BF16)


def pair_partial_kernel(pos_ref, f_ref, x_ref, z_ref, c_ref, cz_ref, out_ref):
    core1, odd = pos_ref[0] == 1, pos_ref[1] == 1
    two = jnp.where(odd, f_ref[0], f_ref[4])
    far = jnp.where(odd, f_ref[4], f_ref[0])
    side = jnp.where(core1, f_ref[1], f_ref[3])
    own_side = core1 == odd
    fc = jnp.where(own_side, side, 0.0)
    fz = jnp.where(own_side, 0.0, side)
    weighted((two, far, fc, fz), (x_ref, z_ref, c_ref, cz_ref), out_ref)


def core_partial_kernel(pos_ref, f_ref, x_ref, y_ref, z_ref, out_ref):
    core1, odd = pos_ref[0] == 1, pos_ref[1] == 1
    near = jnp.where(core1, f_ref[1], f_ref[3])
    far = jnp.where(core1, f_ref[3], f_ref[1])
    by_pair = core1 == odd
    weighted((near, jnp.where(by_pair, far, 0.0), jnp.where(by_pair, 0.0, far)), (x_ref, y_ref, z_ref), out_ref)


def lesser_window_kernel(pos_ref, f_ref, x_ref, y_ref, z_ref, r_ref, out_ref):
    odd = pos_ref[1] == 1
    fy = jnp.where(odd, f_ref[4], f_ref[0])
    fz = jnp.where(odd, f_ref[0], f_ref[4])
    weighted((f_ref[2], fy, fz, None), (x_ref, y_ref, z_ref, r_ref), out_ref)


def greater_window_kernel(pos_ref, f_ref, x_ref, c_ref, r_ref, out_ref):
    core1 = pos_ref[0] == 1
    weighted((f_ref[2], jnp.where(core1, f_ref[3], f_ref[1]), None), (x_ref, c_ref, r_ref), out_ref)


def combine(kernel, pos, factors, *blocks):
    return pl.pallas_call(
        kernel,
        out_shape=jax.ShapeDtypeStruct(SHAPE, BF16),
        in_specs=[SMEM, SMEM] + [VMEM] * len(blocks),
        out_specs=VMEM,
        compiler_params=PARAMS,
        cost_estimate=pl.CostEstimate(flops=2**21, bytes_accessed=2**21, transcendentals=0),
    )(pos, factors, *blocks)


def sigma_kernel(pos_ref, occ_ref, off_ref, own_ref, a_ref, b_ref, mat_ref, tra_ref, out_ref, ext_ref, acc_ref, *, plus_up):
    swap = pos_ref[2] == 1

    @pl.when(swap)
    def _():
        ext_ref[0:2] = b_ref[...]
        ext_ref[4:6] = a_ref[...]

    @pl.when(jnp.logical_not(swap))
    def _():
        ext_ref[0:2] = a_ref[...]
        ext_ref[4:6] = b_ref[...]

    ext_ref[2:4] = own_ref[...]
    for branch in range(BRANCHES):
        n = occ_ref[branch]
        shift = off_ref[branch]
        up_factor = n + 1.0 if plus_up else n
        down_factor = n if plus_up else n + 1.0
        c = mat_ref[branch]
        t = tra_ref[branch]
        for e in range(2):
            upper = ext_ref[2 + e + shift].astype(F32)
            lower = ext_ref[2 + e - shift].astype(F32)
            mixed = (up_factor * upper + down_factor * lower).astype(BF16)
            left = jnp.dot(c, mixed, preferred_element_type=F32).astype(BF16)
            for h in range(2):
                cols = slice(h * ORB, (h + 1) * ORB)
                right = jnp.dot(left[:, cols], t, preferred_element_type=F32)
                if branch == 0:
                    acc_ref[e, :, cols] = right
                elif branch < BRANCHES - 1:
                    acc_ref[e, :, cols] += right
                else:
                    out_ref[e, :, cols] = (acc_ref[e, :, cols] + right).astype(BF16)


def sigma(pos, occupation, offsets, own, a, b, mats, trans, plus_up):
    return pl.pallas_call(
        functools.partial(sigma_kernel, plus_up=plus_up),
        out_shape=jax.ShapeDtypeStruct(SHAPE, BF16),
        in_specs=[SMEM] * 3 + [VMEM] * 5,
        out_specs=VMEM,
        scratch_shapes=[pltpu.VMEM((6, ORB, 2 * ORB), BF16), pltpu.VMEM(SHAPE, F32)],
        compiler_params=PARAMS,
        cost_estimate=pl.CostEstimate(flops=2**30, bytes_accessed=3 * 2**20, transcendentals=0),
    )(pos, occupation, offsets, own, a, b, mats, trans)


def local(lesser, greater, coupling, occupation, offsets, readers, weights):
    count = lax.axis_size("kz")
    energies = lax.axis_size("en")
    k = lax.axis_index("kz")
    pos = jnp.stack((k & 1, (k >> 1) & 1, lax.axis_index("en") & 1)).astype(jnp.int32)

    def kz(block, route):
        return lax.ppermute(block, "kz", route)

    xl = lesser.reshape(SHAPE)
    xg = greater.reshape(SHAPE)
    mats = coupling[0]
    trans = jnp.swapaxes(mats, 1, 2)
    f = weights * readers[0].astype(F32)

    yl = kz(xl, swap_route(count, 2))
    zg = kz(xg, plane_route(count, -1))
    cg = kz(xg, swap_route(count, 1))
    fy = kz(f, swap_route(count, 2))
    fc = kz(f, swap_route(count, 1))
    yl, f, fy, fc, pos, trans = lax.optimization_barrier((yl, f, fy, fc, pos, trans))
    zl = kz(yl, plane_route(count, 1))
    czg = kz(zg, swap_route(count, 1))
    pg = combine(pair_partial_kernel, pos, fy, xg, zg, cg, czg)
    rg = kz(pg, swap_route(count, 2))
    zl, _ = lax.optimization_barrier((zl, pg))
    ql = combine(core_partial_kernel, pos, fc, xl, yl, zl)
    rl = kz(ql, swap_route(count, 1))
    wl = combine(lesser_window_kernel, pos, f, xl, yl, zl, rl)
    wg = combine(greater_window_kernel, pos, f, xg, cg, rg)

    odd_pairs, even_pairs = pair_route(energies, 1), pair_route(energies, 0)
    bl = lax.ppermute(wl, "en", even_pairs)
    al = lax.ppermute(wl, "en", odd_pairs)
    bg = lax.ppermute(wg, "en", even_pairs)
    ag = lax.ppermute(wg, "en", odd_pairs)
    sl = sigma(pos, occupation, offsets, wl, al, bl, mats, trans, True)
    sg = sigma(pos, occupation, offsets, wg, ag, bg, mats, trans, False)
    return sl.reshape(lesser.shape), sg.reshape(greater.shape)


def solution(mesh):
    wide = P("kz", "en", None, None, None)
    return jax.shard_map(
        local,
        mesh=mesh,
        in_specs=(wide, wide, P(), P(), P(), P("kz", None), P()),
        out_specs=(wide, wide),
        check_vma=False,
    )
```

time: 102 us -> 83.7 us (0.82)
  between operations: 11.1 us -> 0.89 us
  other arithmetic: 8.67 us -> 0.08 us
  starting transfers between devices: 53.2 us -> 45.1 us
  waiting for transfers between devices: 18.5 us -> 25.6 us
  Pallas kernels: 7.29 us -> 10.2 us
  local copies, waits for them, and re-layouts: 2.81 us -> 1.34 us
    convert_element_type x4 -> x0, other arithmetic: 8.66 us -> none  [mix(): return acc.astype(BF16)]
    ppermute x9, waiting for transfers between devices: 5.46 us -> 11.5 us  [kz(): return lax.ppermute(block, 'kz', route)]
    ppermute x9, starting transfers between devices: 37 us -> 31.4 us  [kz(): return lax.ppermute(block, 'kz', route)]
    pallas_call x0 -> x4, Pallas kernels: none -> 3.48 us  [combine(): pl.pallas_call(kernel, out_shape=jax.ShapeDtypeStruct(SHAPE, BF16), in_sp...]
    ppermute x4, starting transfers between devices: 16.2 us -> 13.7 us  [the longest x1 4.96 us: local(): ag = lax.ppermute(wg, 'en', odd_pairs)]
    slice x3 -> x0, local copies, waits for them, and re-layouts: 1.9 us -> none  [the longest x1 0.66 us: local(): f[1]]
    ppermute x4, waiting for transfers between devices: 13 us -> 14.1 us  [the longest x1 6 us: local(): al = lax.ppermute(wl, 'en', odd_pairs)]
  transfers between devices with their start and end apart: 13 -> 13, of which waited for: 4 -> 7; matrix products, arithmetic and copies ran while one was open for 11% -> 2% of each run, Pallas kernels for 3% -> 8%
where the time goes in v2:
time: 83.7 us; the launch traced here: 83.2 us
  starting transfers between devices  45.1 us (54%)
  waiting for transfers between devices  25.6 us (31%)
  Pallas kernels  10.2 us (12%)
  local copies, waits for them, and re-layouts  1.34 us (2%)
  between operations  0.89 us (1%)
    ppermute x9, starting transfers between devices, kz(): return lax.ppermute(block, 'kz', route)  31.4 us
    ppermute x9, waiting for transfers between devices, kz(): return lax.ppermute(block, 'kz', route)  11.5 us
    pallas_call x2, Pallas kernels, sigma(): pl.pallas_call(functools.partial(sigma_kernel, plus_up=plus_up), out_shap...  6.76 us
    ppermute x1, waiting for transfers between devices, local(): al = lax.ppermute(wl, 'en', odd_pairs)  6 us
    ppermute x1, waiting for transfers between devices, local(): ag = lax.ppermute(wg, 'en', odd_pairs)  5.73 us
    ppermute x1, starting transfers between devices, local(): ag = lax.ppermute(wg, 'en', odd_pairs)  4.96 us
    ppermute x1, starting transfers between devices, local(): al = lax.ppermute(wl, 'en', odd_pairs)  4.88 us
    pallas_call x4, Pallas kernels, combine(): pl.pallas_call(kernel, out_shape=jax.ShapeDtypeStruct(SHAPE, BF16), in_sp...  3.48 us
  transfers between devices with their start and end apart: 13, of which 7 were waited for; matrix products, arithmetic and copies ran while one was open for 2% of the time, Pallas kernels for 8%

profile of v2, /device:TPU:6, one launch (start us, length us, event | category | flops | bytes accessed | tf_op | source)
XLA Modules:
  0.0 83.2 jit_solution(6204100416143069209)
XLA Ops:
  0.6 0.0 copy-start.5
  0.6 0.0 copy-start.6
  0.6 11.5 %collective-permute-start.4 = (bf16[2,256,512]{2,1,0:T(8,128)(2,1)}, bf16[2,256,512]{2,1,0:T(8,128)(2,1)S(1)}, u32[]{:S(2)}, u32[]{:S(2)}) collective-permute-start(bf16[2,256,512]{2,1,0:T(8,128)(2,1)} %bitcast.17), channel_id=1, source_target_pairs={{0,480},{8,488},{16,48},{24,56},{32,0},{40,8},{48,80},{56,88},{64,... | collective-permute-start | bytes 1572872 | tf_op jit(solution)/shard_map/ppermute | solution.py:145
  12.2 1.9 %collective-permute-start = (bf16[2,256,512]{2,1,0:T(8,128)(2,1)}, bf16[2,256,512]{2,1,0:T(8,128)(2,1)S(1)}, u32[]{:S(2)}, u32[]{:S(2)}) collective-permute-start(bf16[2,256,512]{2,1,0:T(8,128)(2,1)} %bitcast.21), channel_id=1, source_target_pairs={{0,16},{8,24},{16,0},{24,8},{32,48},{40,56},{48,32},{56,40},{64,80... | collective-permute-start | bytes 1572872 | tf_op jit(solution)/shard_map/ppermute | solution.py:145
  14.1 0.0 copy-done.5
  14.1 0.0 copy-done.6
  14.2 3.9 %collective-permute-start.1 = (f32[5]{0:T(128)S(1)}, f32[5]{0:T(128)S(1)}, u32[]{:S(2)}, u32[]{:S(2)}) collective-permute-start(f32[5]{0:T(128)S(1)} %bitcast_multiply_fusion.f_ref), channel_id=1, source_target_pairs={{0,16},{8,24},{16,0},{24,8},{32,48},{40,56},{48,32},{56,40},{64,80... | collective-permute-start | bytes 68 | tf_op jit(solution)/shard_map/ppermute | solution.py:145
  18.1 1.9 %collective-permute-start.2 = (f32[5]{0:T(128)S(1)}, f32[5]{0:T(128)S(1)}, u32[]{:S(2)}, u32[]{:S(2)}) collective-permute-start(f32[5]{0:T(128)S(1)} %bitcast_multiply_fusion.f_ref), channel_id=1, source_target_pairs={{0,8},{8,0},{16,24},{24,16},{32,40},{40,32},{48,56},{56,48},{64,72... | collective-permute-start | bytes 68 | tf_op jit(solution)/shard_map/ppermute | solution.py:145
  20.0 2.4 %collective-permute-start.5 = (bf16[2,256,512]{2,1,0:T(8,128)(2,1)}, bf16[2,256,512]{2,1,0:T(8,128)(2,1)S(1)}, u32[]{:S(2)}, u32[]{:S(2)}) collective-permute-start(bf16[2,256,512]{2,1,0:T(8,128)(2,1)} %bitcast.18), channel_id=1, source_target_pairs={{0,8},{8,0},{16,24},{24,16},{32,40},{40,32},{48,56},{56,48},{64,72... | collective-permute-start | bytes 1572872 | tf_op jit(solution)/shard_map/ppermute | solution.py:145
  22.4 0.0 copy-start
  22.5 1.3 %copy.9 = bf16[1,4,256,256]{2,3,1,0:T(8,128)(2,1)S(1)} copy(bf16[1,4,256,256]{3,2,1,0:T(8,128)(2,1)} %param.9) | data formatting | bytes 1048576 | tf_op args[2]
  23.8 0.0 collective-permute-done.4.z_ref
  23.8 1.9 %collective-permute-start.6 = (bf16[2,256,512]{2,1,0:T(8,128)(2,1)S(1)}, bf16[2,256,512]{2,1,0:T(8,128)(2,1)S(1)}, u32[]{:S(2)}, u32[]{:S(2)}) collective-permute-start(bf16[2,256,512]{2,1,0:T(8,128)(2,1)S(1)} %collective-permute-done.4.z_ref), channel_id=1, source_target_pairs={{0,8},{8,0},{16,24},{24,16},{32,40},{40,32},{48,56},{56,48},{64,72... | collective-permute-start | bytes 1572872 | tf_op jit(solution)/shard_map/ppermute | solution.py:145
  25.7 0.1 pad_add_fusion.pos_ref
  25.8 2.0 %collective-permute-done.1.f_ref = f32[5]{0:T(128)S(1)} collective-permute-done((f32[5]{0:T(128)S(1)}, f32[5]{0:T(128)S(1)}, u32[]{:S(2)}, u32[]{:S(2)}) %collective-permute-start.1) | collective-permute-done | bytes 52 | tf_op jit(solution)/shard_map/ppermute | solution.py:145
  27.8 0.0 collective-permute-done.2.f_ref
  27.8 0.0 collective-permute-done.y_ref
  27.8 0.0 copy-start.1
  27.8 2.1 %collective-permute-start.3 = (bf16[2,256,512]{2,1,0:T(8,128)(2,1)S(1)}, bf16[2,256,512]{2,1,0:T(8,128)(2,1)S(1)}, u32[]{:S(2)}, u32[]{:S(2)}) collective-permute-start(bf16[2,256,512]{2,1,0:T(8,128)(2,1)S(1)} %collective-permute-done.y_ref), channel_id=1, source_target_pairs={{0,32},{8,40},{16,496},{24,504},{32,64},{40,72},{48,16},{56,24},{6... | collective-permute-start | bytes 1572872 | tf_op jit(solution)/shard_map/ppermute | solution.py:145
  29.8 0.0 collective-permute-done.5.c_ref
  29.8 0.0 collective-permute-done.6.cz_ref
  29.8 0.0 copy-done
  29.9 0.9 %shard_map.86 = bf16[2,256,512]{2,1,0:T(8,128)(2,1)S(1)} custom-call(s32[3]{0:T(128)S(1)} %pad_add_fusion.pos_ref, f32[5]{0:T(128)S(1)} %collective-permute-done.1.f_ref, bf16[2,256,512]{2,1,0:T(8,128)(2,1)S(1)} %bitcast.19, bf16[2,256,512]{2,1,0:T(8,128)(2,1)S(1)} %collective-permute-done.4.z_ref, bf16[2,256,512]{2,1,0:T(8,128)(2,1)S(1)} %collective-permute-done.5.c_ref, ...), custom_call_target="tpu_custom_call" | custom-call | flops 2097152 | bytes 2097152 | tf_op jit(solution)/shard_map/pallas_call | solution.py:79
  30.8 3.8 %collective-permute-start.10 = (bf16[2,256,512]{2,1,0:T(8,128)(2,1)S(1)}, bf16[2,256,512]{2,1,0:T(8,128)(2,1)S(1)}, u32[]{:S(2)}, u32[]{:S(2)}) collective-permute-start(bf16[2,256,512]{2,1,0:T(8,128)(2,1)S(1)} %shard_map.86), channel_id=1, source_target_pairs={{0,16},{8,24},{16,0},{24,8},{32,48},{40,56},{48,32},{56,40},{64,80... | collective-permute-start | bytes 1572872 | tf_op jit(solution)/shard_map/ppermute | solution.py:145
  34.6 9.3 %collective-permute-done.3.z_ref = bf16[2,256,512]{2,1,0:T(8,128)(2,1)S(1)} collective-permute-done((bf16[2,256,512]{2,1,0:T(8,128)(2,1)S(1)}, bf16[2,256,512]{2,1,0:T(8,128)(2,1)S(1)}, u32[]{:S(2)}, u32[]{:S(2)}) %collective-permute-start.3) | collective-permute-done | bytes 524320 | tf_op jit(solution)/shard_map/ppermute | solution.py:145
  43.9 0.0 copy-done.1
  43.9 0.8 %shard_map.87 = bf16[2,256,512]{2,1,0:T(8,128)(2,1)S(1)} custom-call(s32[3]{0:T(128)S(1)} %pad_add_fusion.pos_ref, f32[5]{0:T(128)S(1)} %collective-permute-done.2.f_ref, bf16[2,256,512]{2,1,0:T(8,128)(2,1)S(1)} %bitcast.22, bf16[2,256,512]{2,1,0:T(8,128)(2,1)S(1)} %collective-permute-done.y_ref, bf16[2,256,512]{2,1,0:T(8,128)(2,1)S(1)} %collective-permute-done.3.z_ref), custom_call_target="tpu_custom_call" | custom-call | flops 2097152 | bytes 2097152 | tf_op jit(solution)/shard_map/pallas_call | solution.py:79
  44.7 1.9 %collective-permute-start.7 = (bf16[2,256,512]{2,1,0:T(8,128)(2,1)S(1)}, bf16[2,256,512]{2,1,0:T(8,128)(2,1)S(1)}, u32[]{:S(2)}, u32[]{:S(2)}) collective-permute-start(bf16[2,256,512]{2,1,0:T(8,128)(2,1)S(1)} %shard_map.87), channel_id=1, source_target_pairs={{0,8},{8,0},{16,24},{24,16},{32,40},{40,32},{48,56},{56,48},{64,72... | collective-permute-start | bytes 1572872 | tf_op jit(solution)/shard_map/ppermute | solution.py:145
  46.7 0.2 collective-permute-done.10.r_ref
  46.9 0.8 shard_map.90.own_ref
  47.7 0.0 copy-start.2
  47.7 5.0 %collective-permute-start.11 = (bf16[2,256,512]{2,1,0:T(8,128)(2,1)S(1)}, bf16[2,256,512]{2,1,0:T(8,128)(2,1)S(1)}, u32[]{:S(2)}, u32[]{:S(2)}) collective-permute-start(bf16[2,256,512]{2,1,0:T(8,128)(2,1)S(1)} %shard_map.90.own_ref), channel_id=1, source_target_pairs={{1,2},{3,4},{5,6},{2,1},{4,3},{6,5},{9,10},{11,12},{13,14},{10,9},... | collective-permute-start | bytes 1572872 | tf_op jit(solution)/shard_map/ppermute | solution.py:173
  52.7 1.9 %collective-permute-start.12 = (bf16[2,256,512]{2,1,0:T(8,128)(2,1)S(1)}, bf16[2,256,512]{2,1,0:T(8,128)(2,1)S(1)}, u32[]{:S(2)}, u32[]{:S(2)}) collective-permute-start(bf16[2,256,512]{2,1,0:T(8,128)(2,1)S(1)} %shard_map.90.own_ref), channel_id=1, source_target_pairs={{0,1},{2,3},{4,5},{6,7},{1,0},{3,2},{5,4},{7,6},{8,9},{10,11},{12,... | collective-permute-start | bytes 1572872 | tf_op jit(solution)/shard_map/ppermute | solution.py:172
  54.6 0.0 collective-permute-done.7.r_ref
  54.6 0.9 %shard_map.88.own_ref = bf16[2,256,512]{2,1,0:T(8,128)(2,1)S(1)} custom-call(s32[3]{0:T(128)S(1)} %pad_add_fusion.pos_ref, f32[5]{0:T(128)S(1)} %bitcast_multiply_fusion.f_ref, bf16[2,256,512]{2,1,0:T(8,128)(2,1)S(1)} %bitcast.23, bf16[2,256,512]{2,1,0:T(8,128)(2,1)S(1)} %collective-permute-done.y_ref, ...), custom_call_target="tpu_custom_call" | custom-call | flops 2097152 | bytes 2097152 | tf_op jit(solution)/shard_map/pallas_call | solution.py:79
  55.5 0.0 copy-start.3
  55.5 0.0 copy-start.4
  55.5 4.9 %collective-permute-start.8 = (bf16[2,256,512]{2,1,0:T(8,128)(2,1)S(1)}, bf16[2,256,512]{2,1,0:T(8,128)(2,1)S(1)}, u32[]{:S(2)}, u32[]{:S(2)}) collective-permute-start(bf16[2,256,512]{2,1,0:T(8,128)(2,1)S(1)} %shard_map.88.own_ref), channel_id=1, source_target_pairs={{1,2},{3,4},{5,6},{2,1},{4,3},{6,5},{9,10},{11,12},{13,14},{10,9},... | collective-permute-start | bytes 1572872 | tf_op jit(solution)/shard_map/ppermute | solution.py:171
  60.4 1.9 %collective-permute-start.9 = (bf16[2,256,512]{2,1,0:T(8,128)(2,1)S(1)}, bf16[2,256,512]{2,1,0:T(8,128)(2,1)S(1)}, u32[]{:S(2)}, u32[]{:S(2)}) collective-permute-start(bf16[2,256,512]{2,1,0:T(8,128)(2,1)S(1)} %shard_map.88.own_ref), channel_id=1, source_target_pairs={{0,1},{2,3},{4,5},{6,7},{1,0},{3,2},{5,4},{7,6},{8,9},{10,11},{12,... | collective-permute-start | bytes 1572872 | tf_op jit(solution)/shard_map/ppermute | solution.py:170
  62.3 5.7 %collective-permute-done.11.a_ref = bf16[2,256,512]{2,1,0:T(8,128)(2,1)S(1)} collective-permute-done((bf16[2,256,512]{2,1,0:T(8,128)(2,1)S(1)}, bf16[2,256,512]{2,1,0:T(8,128)(2,1)S(1)}, u32[]{:S(2)}, u32[]{:S(2)}) %collective-permute-start.11) | collective-permute-done | bytes 524320 | tf_op jit(solution)/shard_map/ppermute | solution.py:173
  68.1 1.2 %collective-permute-done.12.b_ref = bf16[2,256,512]{2,1,0:T(8,128)(2,1)S(1)} collective-permute-done((bf16[2,256,512]{2,1,0:T(8,128)(2,1)S(1)}, bf16[2,256,512]{2,1,0:T(8,128)(2,1)S(1)}, u32[]{:S(2)}, u32[]{:S(2)}) %collective-permute-start.12) | collective-permute-done | bytes 524320 | tf_op jit(solution)/shard_map/ppermute | solution.py:172
  69.3 0.0 copy-done.2
  69.3 0.0 copy-done.3
  69.3 0.0 copy-done.4
  69.3 3.4 %shard_map.91 = bf16[2,256,512]{2,1,0:T(8,128)(2,1)} custom-call(s32[3]{0:T(128)S(1)} %pad_add_fusion.pos_ref, f32[4]{0:T(128)S(1)} %copy-done.3, s32[4]{0:T(128)S(1)} %copy-done.4, bf16[2,256,512]{2,1,0:T(8,128)(2,1)S(1)} %shard_map.90.own_ref, bf16[2,256,512]{2,1,0:T(8,128)(2,1)S(1)} %collective-permute-done.11.a_ref, ...), custom_call_target="tpu_custom_call" | custom-call | flops 1073741824 | bytes 3145728 | tf_op jit(solution)/shard_map/pallas_call | solution.py:127
  72.7 6.0 %collective-permute-done.8.a_ref = bf16[2,256,512]{2,1,0:T(8,128)(2,1)S(1)} collective-permute-done((bf16[2,256,512]{2,1,0:T(8,128)(2,1)S(1)}, bf16[2,256,512]{2,1,0:T(8,128)(2,1)S(1)}, u32[]{:S(2)}, u32[]{:S(2)}) %collective-permute-start.8) | collective-permute-done | bytes 524320 | tf_op jit(solution)/shard_map/ppermute | solution.py:171
  78.7 1.1 %collective-permute-done.9.b_ref = bf16[2,256,512]{2,1,0:T(8,128)(2,1)S(1)} collective-permute-done((bf16[2,256,512]{2,1,0:T(8,128)(2,1)S(1)}, bf16[2,256,512]{2,1,0:T(8,128)(2,1)S(1)}, u32[]{:S(2)}, u32[]{:S(2)}) %collective-permute-start.9) | collective-permute-done | bytes 524320 | tf_op jit(solution)/shard_map/ppermute | solution.py:170
  79.8 3.4 %shard_map.89 = bf16[2,256,512]{2,1,0:T(8,128)(2,1)} custom-call(s32[3]{0:T(128)S(1)} %pad_add_fusion.pos_ref, f32[4]{0:T(128)S(1)} %copy-done.3, s32[4]{0:T(128)S(1)} %copy-done.4, bf16[2,256,512]{2,1,0:T(8,128)(2,1)S(1)} %shard_map.88.own_ref, bf16[2,256,512]{2,1,0:T(8,128)(2,1)S(1)} %collective-permute-done.8.a_ref, ...), custom_call_target="tpu_custom_call" | custom-call | flops 1073741824 | bytes 3145728 | tf_op jit(solution)/shard_map/pallas_call | solution.py:127
  (1 shorter events, 0.0 us)
Async XLA Ops:
  0.6 13.5 %copy-start.5 = (f32[5]{0:T(128)S(1)}, f32[5]{0:T(128)}, u32[]{:S(2)}) copy-start(f32[5]{0:T(128)} %param.13) | copy-start | bytes 64
  0.6 13.5 %copy-start.6 = (s32[1,5]{1,0:T(1,128)S(1)}, s32[1,5]{1,0:T(1,128)}, u32[]{:S(2)}) copy-start(s32[1,5]{1,0:T(1,128)} %param.12) | copy-start | bytes 64
  0.6 23.1 %collective-permute-start.4 = (bf16[2,256,512]{2,1,0:T(8,128)(2,1)}, bf16[2,256,512]{2,1,0:T(8,128)(2,1)S(1)}, u32[]{:S(2)}, u32[]{:S(2)}) collective-permute-start(bf16[2,256,512]{2,1,0:T(8,128)(2,1)} %bitcast.17), channel_id=1, source_target_pairs={{0,480},{8,488},{16,48},{24,56},{32,0},{40,8},{48,80},{56,88},{64,... | collective-permute-start | bytes 1572872 | tf_op jit(solution)/shard_map/ppermute | solution.py:145
  12.2 15.6 %collective-permute-start = (bf16[2,256,512]{2,1,0:T(8,128)(2,1)}, bf16[2,256,512]{2,1,0:T(8,128)(2,1)S(1)}, u32[]{:S(2)}, u32[]{:S(2)}) collective-permute-start(bf16[2,256,512]{2,1,0:T(8,128)(2,1)} %bitcast.21), channel_id=1, source_target_pairs={{0,16},{8,24},{16,0},{24,8},{32,48},{40,56},{48,32},{56,40},{64,80... | collective-permute-start | bytes 1572872 | tf_op jit(solution)/shard_map/ppermute | solution.py:145
  14.2 13.6 %collective-permute-start.1 = (f32[5]{0:T(128)S(1)}, f32[5]{0:T(128)S(1)}, u32[]{:S(2)}, u32[]{:S(2)}) collective-permute-start(f32[5]{0:T(128)S(1)} %bitcast_multiply_fusion.f_ref), channel_id=1, source_target_pairs={{0,16},{8,24},{16,0},{24,8},{32,48},{40,56},{48,32},{56,40},{64,80... | collective-permute-start | bytes 68 | tf_op jit(solution)/shard_map/ppermute | solution.py:145
  18.1 9.7 %collective-permute-start.2 = (f32[5]{0:T(128)S(1)}, f32[5]{0:T(128)S(1)}, u32[]{:S(2)}, u32[]{:S(2)}) collective-permute-start(f32[5]{0:T(128)S(1)} %bitcast_multiply_fusion.f_ref), channel_id=1, source_target_pairs={{0,8},{8,0},{16,24},{24,16},{32,40},{40,32},{48,56},{56,48},{64,72... | collective-permute-start | bytes 68 | tf_op jit(solution)/shard_map/ppermute | solution.py:145
  20.0 9.8 %collective-permute-start.5 = (bf16[2,256,512]{2,1,0:T(8,128)(2,1)}, bf16[2,256,512]{2,1,0:T(8,128)(2,1)S(1)}, u32[]{:S(2)}, u32[]{:S(2)}) collective-permute-start(bf16[2,256,512]{2,1,0:T(8,128)(2,1)} %bitcast.18), channel_id=1, source_target_pairs={{0,8},{8,0},{16,24},{24,16},{32,40},{40,32},{48,56},{56,48},{64,72... | collective-permute-start | bytes 1572872 | tf_op jit(solution)/shard_map/ppermute | solution.py:145
  22.4 7.4 %copy-start = (bf16[1,2,1,256,512]{4,3,2,1,0:T(8,128)(2,1)S(1)}, bf16[1,2,1,256,512]{4,3,2,1,0:T(8,128)(2,1)}, u32[]{:S(2)}) copy-start(bf16[1,2,1,256,512]{4,3,2,1,0:T(8,128)(2,1)} %param.8) | copy-start | bytes 1572868
  23.8 6.1 %collective-permute-start.6 = (bf16[2,256,512]{2,1,0:T(8,128)(2,1)S(1)}, bf16[2,256,512]{2,1,0:T(8,128)(2,1)S(1)}, u32[]{:S(2)}, u32[]{:S(2)}) collective-permute-start(bf16[2,256,512]{2,1,0:T(8,128)(2,1)S(1)} %collective-permute-done.4.z_ref), channel_id=1, source_target_pairs={{0,8},{8,0},{16,24},{24,16},{32,40},{40,32},{48,56},{56,48},{64,72... | collective-permute-start | bytes 1572872 | tf_op jit(solution)/shard_map/ppermute | solution.py:145
  27.8 16.1 %copy-start.1 = (bf16[1,2,1,256,512]{4,3,2,1,0:T(8,128)(2,1)S(1)}, bf16[1,2,1,256,512]{4,3,2,1,0:T(8,128)(2,1)}, u32[]{:S(2)}) copy-start(bf16[1,2,1,256,512]{4,3,2,1,0:T(8,128)(2,1)} %param.7) | copy-start | bytes 1572868
  27.8 16.1 %collective-permute-start.3 = (bf16[2,256,512]{2,1,0:T(8,128)(2,1)S(1)}, bf16[2,256,512]{2,1,0:T(8,128)(2,1)S(1)}, u32[]{:S(2)}, u32[]{:S(2)}) collective-permute-start(bf16[2,256,512]{2,1,0:T(8,128)(2,1)S(1)} %collective-permute-done.y_ref), channel_id=1, source_target_pairs={{0,32},{8,40},{16,496},{24,504},{32,64},{40,72},{48,16},{56,24},{6... | collective-permute-start | bytes 1572872 | tf_op jit(solution)/shard_map/ppermute | solution.py:145
  30.8 16.1 %collective-permute-start.10 = (bf16[2,256,512]{2,1,0:T(8,128)(2,1)S(1)}, bf16[2,256,512]{2,1,0:T(8,128)(2,1)S(1)}, u32[]{:S(2)}, u32[]{:S(2)}) collective-permute-start(bf16[2,256,512]{2,1,0:T(8,128)(2,1)S(1)} %shard_map.86), channel_id=1, source_target_pairs={{0,16},{8,24},{16,0},{24,8},{32,48},{40,56},{48,32},{56,40},{64,80... | collective-permute-start | bytes 1572872 | tf_op jit(solution)/shard_map/ppermute | solution.py:145
  44.7 9.8 %collective-permute-start.7 = (bf16[2,256,512]{2,1,0:T(8,128)(2,1)S(1)}, bf16[2,256,512]{2,1,0:T(8,128)(2,1)S(1)}, u32[]{:S(2)}, u32[]{:S(2)}) collective-permute-start(bf16[2,256,512]{2,1,0:T(8,128)(2,1)S(1)} %shard_map.87), channel_id=1, source_target_pairs={{0,8},{8,0},{16,24},{24,16},{32,40},{40,32},{48,56},{56,48},{64,72... | collective-permute-start | bytes 1572872 | tf_op jit(solution)/shard_map/ppermute | solution.py:145
  47.7 21.6 %copy-start.2 = (bf16[1,4,256,256]{3,2,1,0:T(8,128)(2,1)S(1)}, bf16[1,4,256,256]{3,2,1,0:T(8,128)(2,1)}, u32[]{:S(2)}) copy-start(bf16[1,4,256,256]{3,2,1,0:T(8,128)(2,1)} %param.9) | copy-start | bytes 1572868
  47.7 20.4 %collective-permute-start.11 = (bf16[2,256,512]{2,1,0:T(8,128)(2,1)S(1)}, bf16[2,256,512]{2,1,0:T(8,128)(2,1)S(1)}, u32[]{:S(2)}, u32[]{:S(2)}) collective-permute-start(bf16[2,256,512]{2,1,0:T(8,128)(2,1)S(1)} %shard_map.90.own_ref), channel_id=1, source_target_pairs={{1,2},{3,4},{5,6},{2,1},{4,3},{6,5},{9,10},{11,12},{13,14},{10,9},... | collective-permute-start | bytes 1572872 | tf_op jit(solution)/shard_map/ppermute | solution.py:173
  52.7 16.7 %collective-permute-start.12 = (bf16[2,256,512]{2,1,0:T(8,128)(2,1)S(1)}, bf16[2,256,512]{2,1,0:T(8,128)(2,1)S(1)}, u32[]{:S(2)}, u32[]{:S(2)}) collective-permute-start(bf16[2,256,512]{2,1,0:T(8,128)(2,1)S(1)} %shard_map.90.own_ref), channel_id=1, source_target_pairs={{0,1},{2,3},{4,5},{6,7},{1,0},{3,2},{5,4},{7,6},{8,9},{10,11},{12,... | collective-permute-start | bytes 1572872 | tf_op jit(solution)/shard_map/ppermute | solution.py:172
  55.5 13.8 %copy-start.3 = (f32[4]{0:T(128)S(1)}, f32[4]{0:T(128)}, u32[]{:S(2)}) copy-start(f32[4]{0:T(128)} %occ_ref.3) | copy-start | bytes 52
  55.5 13.8 %copy-start.4 = (s32[4]{0:T(128)S(1)}, s32[4]{0:T(128)}, u32[]{:S(2)}) copy-start(s32[4]{0:T(128)} %off_ref.3) | copy-start | bytes 52
  55.5 23.2 %collective-permute-start.8 = (bf16[2,256,512]{2,1,0:T(8,128)(2,1)S(1)}, bf16[2,256,512]{2,1,0:T(8,128)(2,1)S(1)}, u32[]{:S(2)}, u32[]{:S(2)}) collective-permute-start(bf16[2,256,512]{2,1,0:T(8,128)(2,1)S(1)} %shard_map.88.own_ref), channel_id=1, source_target_pairs={{1,2},{3,4},{5,6},{2,1},{4,3},{6,5},{9,10},{11,12},{13,14},{10,9},... | collective-permute-start | bytes 1572872 | tf_op jit(solution)/shard_map/ppermute | solution.py:171
  60.4 19.4 %collective-permute-start.9 = (bf16[2,256,512]{2,1,0:T(8,128)(2,1)S(1)}, bf16[2,256,512]{2,1,0:T(8,128)(2,1)S(1)}, u32[]{:S(2)}, u32[]{:S(2)}) collective-permute-start(bf16[2,256,512]{2,1,0:T(8,128)(2,1)S(1)} %shard_map.88.own_ref), channel_id=1, source_target_pairs={{0,1},{2,3},{4,5},{6,7},{1,0},{3,2},{5,4},{7,6},{8,9},{10,11},{12,... | collective-permute-start | bytes 1572872 | tf_op jit(solution)/shard_map/ppermute | solution.py:170

commit v3 on v2

--- a/solution.py
+++ b/solution.py
@@ -63,16 +63,16 @@
     weighted((near, jnp.where(by_pair, far, 0.0), jnp.where(by_pair, 0.0, far)), (x_ref, y_ref, z_ref), out_ref)
 
 
+def greater_window_kernel(pos_ref, f_ref, x_ref, c_ref, r_ref, out_ref):
+    core1 = pos_ref[0] == 1
+    weighted((f_ref[2], jnp.where(core1, f_ref[3], f_ref[1]), None), (x_ref, c_ref, r_ref), out_ref)
+
+
 def lesser_window_kernel(pos_ref, f_ref, x_ref, y_ref, z_ref, r_ref, out_ref):
     odd = pos_ref[1] == 1
     fy = jnp.where(odd, f_ref[4], f_ref[0])
     fz = jnp.where(odd, f_ref[0], f_ref[4])
     weighted((f_ref[2], fy, fz, None), (x_ref, y_ref, z_ref, r_ref), out_ref)
-
-
-def greater_window_kernel(pos_ref, f_ref, x_ref, c_ref, r_ref, out_ref):
-    core1 = pos_ref[0] == 1
-    weighted((f_ref[2], jnp.where(core1, f_ref[3], f_ref[1]), None), (x_ref, c_ref, r_ref), out_ref)
 
 
 def combine(kernel, pos, factors, *blocks):
@@ -86,53 +86,65 @@
     )(pos, factors, *blocks)
 
 
-def sigma_kernel(pos_ref, occ_ref, off_ref, own_ref, a_ref, b_ref, mat_ref, tra_ref, out_ref, ext_ref, acc_ref, *, plus_up):
-    swap = pos_ref[2] == 1
-
-    @pl.when(swap)
-    def _():
-        ext_ref[0:2] = b_ref[...]
-        ext_ref[4:6] = a_ref[...]
-
-    @pl.when(jnp.logical_not(swap))
-    def _():
-        ext_ref[0:2] = a_ref[...]
-        ext_ref[4:6] = b_ref[...]
-
-    ext_ref[2:4] = own_ref[...]
+def stage_kernel(a_ref, b_ref, c_ref, d_ref):
+    c_ref[...] = a_ref[...]
+    d_ref[...] = b_ref[...]
+
+
+def stage(a, b):
+    shape = jax.ShapeDtypeStruct(SHAPE, BF16)
+    return pl.pallas_call(
+        stage_kernel, out_shape=[shape, shape], in_specs=[VMEM, VMEM], out_specs=[VMEM, VMEM], compiler_params=PARAMS
+    )(a, b)
+
+
+def sigma_part(occ_ref, off_ref, own_ref, below_ref, above_ref, mat_ref, e, cols, plus_up):
+    acc = None
     for branch in range(BRANCHES):
         n = occ_ref[branch]
-        shift = off_ref[branch]
+        one = off_ref[branch] == 1
         up_factor = n + 1.0 if plus_up else n
         down_factor = n if plus_up else n + 1.0
-        c = mat_ref[branch]
-        t = tra_ref[branch]
+        if e == 0:
+            upper = jnp.where(one, own_ref[1, :, cols], above_ref[0, :, cols])
+            lower = jnp.where(one, below_ref[1, :, cols], below_ref[0, :, cols])
+        else:
+            upper = jnp.where(one, above_ref[0, :, cols], above_ref[1, :, cols])
+            lower = jnp.where(one, own_ref[0, :, cols], below_ref[1, :, cols])
+        mixed = (up_factor * upper.astype(F32) + down_factor * lower.astype(F32)).astype(BF16)
+        left = jnp.dot(mat_ref[branch], mixed, preferred_element_type=F32).astype(BF16)
+        right = lax.dot_general(left, mat_ref[branch], (((1,), (1,)), ((), ())), preferred_element_type=F32)
+        acc = right if acc is None else acc + right
+    return acc.astype(BF16)
+
+
+def by_parity(pos_ref, a_ref, b_ref, body):
+    swap = pos_ref[2] == 1
+    pl.when(swap)(lambda: body(b_ref, a_ref))
+    pl.when(jnp.logical_not(swap))(lambda: body(a_ref, b_ref))
+
+
+def sigma_kernel(pos_ref, occ_ref, off_ref, own_ref, b_ref, a_ref, mat_ref, out_ref, *, plus_up):
+    def body(below_ref, above_ref):
         for e in range(2):
-            upper = ext_ref[2 + e + shift].astype(F32)
-            lower = ext_ref[2 + e - shift].astype(F32)
-            mixed = (up_factor * upper + down_factor * lower).astype(BF16)
-            left = jnp.dot(c, mixed, preferred_element_type=F32).astype(BF16)
             for h in range(2):
                 cols = slice(h * ORB, (h + 1) * ORB)
-                right = jnp.dot(left[:, cols], t, preferred_element_type=F32)
-                if branch == 0:
-                    acc_ref[e, :, cols] = right
-                elif branch < BRANCHES - 1:
-                    acc_ref[e, :, cols] += right
-                else:
-                    out_ref[e, :, cols] = (acc_ref[e, :, cols] + right).astype(BF16)
-
-
-def sigma(pos, occupation, offsets, own, a, b, mats, trans, plus_up):
+                out_ref[e, :, cols] = sigma_part(
+                    occ_ref, off_ref, own_ref, below_ref, above_ref, mat_ref, e, cols, plus_up
+                )
+
+    by_parity(pos_ref, a_ref, b_ref, body)
+
+
+def sigma(plus_up, pos, occupation, offsets, *blocks):
     return pl.pallas_call(
         functools.partial(sigma_kernel, plus_up=plus_up),
         out_shape=jax.ShapeDtypeStruct(SHAPE, BF16),
-        in_specs=[SMEM] * 3 + [VMEM] * 5,
+        in_specs=[SMEM] * 3 + [VMEM] * len(blocks),
         out_specs=VMEM,
-        scratch_shapes=[pltpu.VMEM((6, ORB, 2 * ORB), BF16), pltpu.VMEM(SHAPE, F32)],
         compiler_params=PARAMS,
         cost_estimate=pl.CostEstimate(flops=2**30, bytes_accessed=3 * 2**20, transcendentals=0),
-    )(pos, occupation, offsets, own, a, b, mats, trans)
+    )(pos, occupation, offsets, *blocks)
 
 
 def local(lesser, greater, coupling, occupation, offsets, readers, weights):
@@ -147,32 +159,33 @@
     xl = lesser.reshape(SHAPE)
     xg = greater.reshape(SHAPE)
     mats = coupling[0]
-    trans = jnp.swapaxes(mats, 1, 2)
+    xlv, xgv = stage(xl, xg)
     f = weights * readers[0].astype(F32)
 
     yl = kz(xl, swap_route(count, 2))
     zg = kz(xg, plane_route(count, -1))
     cg = kz(xg, swap_route(count, 1))
     fy = kz(f, swap_route(count, 2))
-    fc = kz(f, swap_route(count, 1))
-    yl, f, fy, fc, pos, trans = lax.optimization_barrier((yl, f, fy, fc, pos, trans))
+    yl, f, fy, pos, xlv, xgv = lax.optimization_barrier((yl, f, fy, pos, xlv, xgv))
     zl = kz(yl, plane_route(count, 1))
     czg = kz(zg, swap_route(count, 1))
-    pg = combine(pair_partial_kernel, pos, fy, xg, zg, cg, czg)
+    pg = combine(pair_partial_kernel, pos, fy, xgv, zg, cg, czg)
     rg = kz(pg, swap_route(count, 2))
-    zl, _ = lax.optimization_barrier((zl, pg))
-    ql = combine(core_partial_kernel, pos, fc, xl, yl, zl)
+    late, _ = lax.optimization_barrier((f, pg))
+    fc = kz(late, swap_route(count, 1))
+    zl, fc = lax.optimization_barrier((zl, fc))
+    ql = combine(core_partial_kernel, pos, fc, xlv, yl, zl)
     rl = kz(ql, swap_route(count, 1))
-    wl = combine(lesser_window_kernel, pos, f, xl, yl, zl, rl)
-    wg = combine(greater_window_kernel, pos, f, xg, cg, rg)
+    wg = combine(greater_window_kernel, pos, f, xgv, cg, rg)
+    wl = combine(lesser_window_kernel, pos, f, xlv, yl, zl, rl)
 
     odd_pairs, even_pairs = pair_route(energies, 1), pair_route(energies, 0)
     bl = lax.ppermute(wl, "en", even_pairs)
     al = lax.ppermute(wl, "en", odd_pairs)
     bg = lax.ppermute(wg, "en", even_pairs)
     ag = lax.ppermute(wg, "en", odd_pairs)
-    sl = sigma(pos, occupation, offsets, wl, al, bl, mats, trans, True)
-    sg = sigma(pos, occupation, offsets, wg, ag, bg, mats, trans, False)
+    sl = sigma(True, pos, occupation, offsets, wl, bl, al, mats)
+    sg = sigma(False, pos, occupation, offsets, wg, bg, ag, mats)
     return sl.reshape(lesser.shape), sg.reshape(greater.shape)
 
 

time: 83.7 us -> 83.2 us (level)
    pallas_call x2, Pallas kernels: 6.76 us -> 5.91 us  [sigma(): pl.pallas_call(functools.partial(sigma_kernel, plus_up=plus_up), out_shap...]
    unnamed x15 -> x14, local copies, waits for them, and re-layouts: 1.34 us -> 2.11 us
  transfers between devices with their start and end apart: 13 -> 13, of which waited for: 7 -> 8; matrix products, arithmetic and copies ran while one was open for 2% -> 0% of each run, Pallas kernels for 8% -> 8%
where the time goes in v3:
time: 83.2 us; the launch traced here: 82.6 us
  starting transfers between devices  44.4 us (53%)
  waiting for transfers between devices  25.7 us (31%)
  Pallas kernels  9.45 us (11%)
  local copies, waits for them, and re-layouts  2.11 us (3%)
  between operations  0.88 us (1%)
    ppermute x9, starting transfers between devices, kz(): return lax.ppermute(block, 'kz', route)  30.7 us
    ppermute x9, waiting for transfers between devices, kz(): return lax.ppermute(block, 'kz', route)  11.2 us
    ppermute x1, waiting for transfers between devices, local(): al = lax.ppermute(wl, 'en', odd_pairs)  6.43 us
    pallas_call x2, Pallas kernels, sigma(): pl.pallas_call(functools.partial(sigma_kernel, plus_up=plus_up), out_shap...  5.91 us
    ppermute x1, waiting for transfers between devices, local(): ag = lax.ppermute(wg, 'en', odd_pairs)  5.72 us
    ppermute x1, starting transfers between devices, local(): ag = lax.ppermute(wg, 'en', odd_pairs)  4.97 us
    ppermute x1, starting transfers between devices, local(): al = lax.ppermute(wl, 'en', odd_pairs)  4.88 us
    pallas_call x4, Pallas kernels, combine(): pl.pallas_call(kernel, out_shape=jax.ShapeDtypeStruct(SHAPE, BF16), in_sp...  3.48 us
  transfers between devices with their start and end apart: 13, of which 8 were waited for; matrix products, arithmetic and copies ran while one was open for 0% of the time, Pallas kernels for 8%

profile of v3, /device:TPU:6, one launch (start us, length us, event | category | flops | bytes accessed | tf_op | source)
XLA Modules:
  0.0 82.6 jit_solution(8028321750205790686)
XLA Ops:
  0.6 0.0 copy-start.5
  0.6 0.0 copy-start.6
  0.6 11.5 %collective-permute-start.3 = (bf16[2,256,512]{2,1,0:T(8,128)(2,1)}, bf16[2,256,512]{2,1,0:T(8,128)(2,1)S(1)}, u32[]{:S(2)}, u32[]{:S(2)}) collective-permute-start(bf16[2,256,512]{2,1,0:T(8,128)(2,1)} %bitcast.16), channel_id=1, source_target_pairs={{0,480},{8,488},{16,48},{24,56},{32,0},{40,8},{48,80},{56,88},{64,... | collective-permute-start | bytes 1572872 | tf_op jit(solution)/shard_map/ppermute | solution.py:157
  12.2 1.9 %collective-permute-start = (bf16[2,256,512]{2,1,0:T(8,128)(2,1)}, bf16[2,256,512]{2,1,0:T(8,128)(2,1)S(1)}, u32[]{:S(2)}, u32[]{:S(2)}) collective-permute-start(bf16[2,256,512]{2,1,0:T(8,128)(2,1)} %bitcast.14), channel_id=1, source_target_pairs={{0,16},{8,24},{16,0},{24,8},{32,48},{40,56},{48,32},{56,40},{64,80... | collective-permute-start | bytes 1572872 | tf_op jit(solution)/shard_map/ppermute | solution.py:157
  14.1 1.9 %collective-permute-start.4 = (bf16[2,256,512]{2,1,0:T(8,128)(2,1)}, bf16[2,256,512]{2,1,0:T(8,128)(2,1)S(1)}, u32[]{:S(2)}, u32[]{:S(2)}) collective-permute-start(bf16[2,256,512]{2,1,0:T(8,128)(2,1)} %bitcast.17), channel_id=1, source_target_pairs={{0,8},{8,0},{16,24},{24,16},{32,40},{40,32},{48,56},{56,48},{64,72... | collective-permute-start | bytes 1572872 | tf_op jit(solution)/shard_map/ppermute | solution.py:157
  16.1 0.0 copy-done.5
  16.1 0.0 copy-done.6
  16.1 3.9 %collective-permute-start.1 = (f32[5]{0:T(128)S(1)}, f32[5]{0:T(128)S(1)}, u32[]{:S(2)}, u32[]{:S(2)}) collective-permute-start(f32[5]{0:T(128)S(1)} %bitcast_multiply_fusion.f_ref), channel_id=1, source_target_pairs={{0,16},{8,24},{16,0},{24,8},{32,48},{40,56},{48,32},{56,40},{64,80... | collective-permute-start | bytes 68 | tf_op jit(solution)/shard_map/ppermute | solution.py:157
  20.0 0.0 copy-start
  20.0 1.0 %copy-done = bf16[1,2,1,256,512]{4,3,2,1,0:T(8,128)(2,1)S(1)} copy-done((bf16[1,2,1,256,512]{4,3,2,1,0:T(8,128)(2,1)S(1)}, bf16[1,2,1,256,512]{4,3,2,1,0:T(8,128)(2,1)}, u32[]{:S(2)}) %copy-start) | copy-done | bytes 524312
  21.1 0.0 copy-start.1
  21.1 1.0 %copy-done.1 = bf16[1,2,1,256,512]{4,3,2,1,0:T(8,128)(2,1)S(1)} copy-done((bf16[1,2,1,256,512]{4,3,2,1,0:T(8,128)(2,1)S(1)}, bf16[1,2,1,256,512]{4,3,2,1,0:T(8,128)(2,1)}, u32[]{:S(2)}) %copy-start.1) | copy-done | bytes 524312
  22.1 0.1 shard_map.86
  22.2 1.5 %collective-permute-done.3.z_ref = bf16[2,256,512]{2,1,0:T(8,128)(2,1)S(1)} collective-permute-done((bf16[2,256,512]{2,1,0:T(8,128)(2,1)}, bf16[2,256,512]{2,1,0:T(8,128)(2,1)S(1)}, u32[]{:S(2)}, u32[]{:S(2)}) %collective-permute-start.3) | collective-permute-done | bytes 524320 | tf_op jit(solution)/shard_map/ppermute | solution.py:157
  23.7 1.9 %collective-permute-start.5 = (bf16[2,256,512]{2,1,0:T(8,128)(2,1)S(1)}, bf16[2,256,512]{2,1,0:T(8,128)(2,1)S(1)}, u32[]{:S(2)}, u32[]{:S(2)}) collective-permute-start(bf16[2,256,512]{2,1,0:T(8,128)(2,1)S(1)} %collective-permute-done.3.z_ref), channel_id=1, source_target_pairs={{0,8},{8,0},{16,24},{24,16},{32,40},{40,32},{48,56},{56,48},{64,72... | collective-permute-start | bytes 1572872 | tf_op jit(solution)/shard_map/ppermute | solution.py:157
  25.6 0.1 pad_add_fusion.pos_ref
  25.7 2.1 %collective-permute-done.1.f_ref = f32[5]{0:T(128)S(1)} collective-permute-done((f32[5]{0:T(128)S(1)}, f32[5]{0:T(128)S(1)}, u32[]{:S(2)}, u32[]{:S(2)}) %collective-permute-start.1) | collective-permute-done | bytes 52 | tf_op jit(solution)/shard_map/ppermute | solution.py:157
  27.8 0.0 collective-permute-done.y_ref
  27.8 1.9 %collective-permute-start.2 = (bf16[2,256,512]{2,1,0:T(8,128)(2,1)S(1)}, bf16[2,256,512]{2,1,0:T(8,128)(2,1)S(1)}, u32[]{:S(2)}, u32[]{:S(2)}) collective-permute-start(bf16[2,256,512]{2,1,0:T(8,128)(2,1)S(1)} %collective-permute-done.y_ref), channel_id=1, source_target_pairs={{0,32},{8,40},{16,496},{24,504},{32,64},{40,72},{48,16},{56,24},{6... | collective-permute-start | bytes 1572872 | tf_op jit(solution)/shard_map/ppermute | solution.py:157
  29.7 0.0 collective-permute-done.4.c_ref
  29.7 0.0 collective-permute-done.5.cz_ref
  29.7 0.9 %shard_map.87 = bf16[2,256,512]{2,1,0:T(8,128)(2,1)S(1)} custom-call(s32[3]{0:T(128)S(1)} %pad_add_fusion.pos_ref, f32[5]{0:T(128)S(1)} %collective-permute-done.1.f_ref, bf16[2,256,512]{2,1,0:T(8,128)(2,1)S(1)} %get-tuple-element.20.x_ref, bf16[2,256,512]{2,1,0:T(8,128)(2,1)S(1)} %collective-permute-done.3.z_ref, ...), custom_call_target="tpu_custom_call" | custom-call | flops 2097152 | bytes 2097152 | tf_op jit(solution)/shard_map/pallas_call | solution.py:79
  30.6 3.8 %collective-permute-start.10 = (bf16[2,256,512]{2,1,0:T(8,128)(2,1)S(1)}, bf16[2,256,512]{2,1,0:T(8,128)(2,1)S(1)}, u32[]{:S(2)}, u32[]{:S(2)}) collective-permute-start(bf16[2,256,512]{2,1,0:T(8,128)(2,1)S(1)} %shard_map.87), channel_id=1, source_target_pairs={{0,16},{8,24},{16,0},{24,8},{32,48},{40,56},{48,32},{56,40},{64,80... | collective-permute-start | bytes 1572872 | tf_op jit(solution)/shard_map/ppermute | solution.py:157
  34.4 1.9 %collective-permute-start.6 = (f32[5]{0:T(128)S(1)}, f32[5]{0:T(128)S(1)}, u32[]{:S(2)}, u32[]{:S(2)}) collective-permute-start(f32[5]{0:T(128)S(1)} %bitcast_multiply_fusion.f_ref), channel_id=1, source_target_pairs={{0,8},{8,0},{16,24},{24,16},{32,40},{40,32},{48,56},{56,48},{64,72... | collective-permute-start | bytes 68 | tf_op jit(solution)/shard_map/ppermute | solution.py:157
  36.3 7.4 %collective-permute-done.2.z_ref = bf16[2,256,512]{2,1,0:T(8,128)(2,1)S(1)} collective-permute-done((bf16[2,256,512]{2,1,0:T(8,128)(2,1)S(1)}, bf16[2,256,512]{2,1,0:T(8,128)(2,1)S(1)}, u32[]{:S(2)}, u32[]{:S(2)}) %collective-permute-start.2) | collective-permute-done | bytes 524320 | tf_op jit(solution)/shard_map/ppermute | solution.py:157
  43.7 0.0 collective-permute-done.6.f_ref
  43.7 0.8 %shard_map.88 = bf16[2,256,512]{2,1,0:T(8,128)(2,1)S(1)} custom-call(s32[3]{0:T(128)S(1)} %pad_add_fusion.pos_ref, f32[5]{0:T(128)S(1)} %collective-permute-done.6.f_ref, bf16[2,256,512]{2,1,0:T(8,128)(2,1)S(1)} %get-tuple-element.17.x_ref, bf16[2,256,512]{2,1,0:T(8,128)(2,1)S(1)} %collective-permute-done.y_ref, ...), custom_call_target="tpu_custom_call" | custom-call | flops 2097152 | bytes 2097152 | tf_op jit(solution)/shard_map/pallas_call | solution.py:79
  44.6 1.9 %collective-permute-start.7 = (bf16[2,256,512]{2,1,0:T(8,128)(2,1)S(1)}, bf16[2,256,512]{2,1,0:T(8,128)(2,1)S(1)}, u32[]{:S(2)}, u32[]{:S(2)}) collective-permute-start(bf16[2,256,512]{2,1,0:T(8,128)(2,1)S(1)} %shard_map.88), channel_id=1, source_target_pairs={{0,8},{8,0},{16,24},{24,16},{32,40},{40,32},{48,56},{56,48},{64,72... | collective-permute-start | bytes 1572872 | tf_op jit(solution)/shard_map/ppermute | solution.py:157
  46.5 0.2 collective-permute-done.10.r_ref
  46.7 0.8 shard_map.91.own_ref
  47.5 0.0 copy-start.2
  47.5 5.0 %collective-permute-start.12 = (bf16[2,256,512]{2,1,0:T(8,128)(2,1)S(1)}, bf16[2,256,512]{2,1,0:T(8,128)(2,1)S(1)}, u32[]{:S(2)}, u32[]{:S(2)}) collective-permute-start(bf16[2,256,512]{2,1,0:T(8,128)(2,1)S(1)} %shard_map.91.own_ref), channel_id=1, source_target_pairs={{1,2},{3,4},{5,6},{2,1},{4,3},{6,5},{9,10},{11,12},{13,14},{10,9},... | collective-permute-start | bytes 1572872 | tf_op jit(solution)/shard_map/ppermute | solution.py:186
  52.5 1.9 %collective-permute-start.11 = (bf16[2,256,512]{2,1,0:T(8,128)(2,1)S(1)}, bf16[2,256,512]{2,1,0:T(8,128)(2,1)S(1)}, u32[]{:S(2)}, u32[]{:S(2)}) collective-permute-start(bf16[2,256,512]{2,1,0:T(8,128)(2,1)S(1)} %shard_map.91.own_ref), channel_id=1, source_target_pairs={{0,1},{2,3},{4,5},{6,7},{1,0},{3,2},{5,4},{7,6},{8,9},{10,11},{12,... | collective-permute-start | bytes 1572872 | tf_op jit(solution)/shard_map/ppermute | solution.py:185
  54.4 0.0 collective-permute-done.7.r_ref
  54.4 0.9 %shard_map.89.own_ref = bf16[2,256,512]{2,1,0:T(8,128)(2,1)S(1)} custom-call(s32[3]{0:T(128)S(1)} %pad_add_fusion.pos_ref, f32[5]{0:T(128)S(1)} %bitcast_multiply_fusion.f_ref, bf16[2,256,512]{2,1,0:T(8,128)(2,1)S(1)} %get-tuple-element.17.x_ref, bf16[2,256,512]{2,1,0:T(8,128)(2,1)S(1)} %collective-permute-done.y_ref, ...), custom_call_target="tpu_custom_call" | custom-call | flops 2097152 | bytes 2097152 | tf_op jit(solution)/shard_map/pallas_call | solution.py:79
  55.4 0.0 copy-start.3
  55.4 0.0 copy-start.4
  55.4 4.9 %collective-permute-start.9 = (bf16[2,256,512]{2,1,0:T(8,128)(2,1)S(1)}, bf16[2,256,512]{2,1,0:T(8,128)(2,1)S(1)}, u32[]{:S(2)}, u32[]{:S(2)}) collective-permute-start(bf16[2,256,512]{2,1,0:T(8,128)(2,1)S(1)} %shard_map.89.own_ref), channel_id=1, source_target_pairs={{1,2},{3,4},{5,6},{2,1},{4,3},{6,5},{9,10},{11,12},{13,14},{10,9},... | collective-permute-start | bytes 1572872 | tf_op jit(solution)/shard_map/ppermute | solution.py:184
  60.3 1.9 %collective-permute-start.8 = (bf16[2,256,512]{2,1,0:T(8,128)(2,1)S(1)}, bf16[2,256,512]{2,1,0:T(8,128)(2,1)S(1)}, u32[]{:S(2)}, u32[]{:S(2)}) collective-permute-start(bf16[2,256,512]{2,1,0:T(8,128)(2,1)S(1)} %shard_map.89.own_ref), channel_id=1, source_target_pairs={{0,1},{2,3},{4,5},{6,7},{1,0},{3,2},{5,4},{7,6},{8,9},{10,11},{12,... | collective-permute-start | bytes 1572872 | tf_op jit(solution)/shard_map/ppermute | solution.py:183
  62.2 5.7 %collective-permute-done.12.a_ref = bf16[2,256,512]{2,1,0:T(8,128)(2,1)S(1)} collective-permute-done((bf16[2,256,512]{2,1,0:T(8,128)(2,1)S(1)}, bf16[2,256,512]{2,1,0:T(8,128)(2,1)S(1)}, u32[]{:S(2)}, u32[]{:S(2)}) %collective-permute-start.12) | collective-permute-done | bytes 524320 | tf_op jit(solution)/shard_map/ppermute | solution.py:186
  67.9 1.2 %collective-permute-done.11.b_ref = bf16[2,256,512]{2,1,0:T(8,128)(2,1)S(1)} collective-permute-done((bf16[2,256,512]{2,1,0:T(8,128)(2,1)S(1)}, bf16[2,256,512]{2,1,0:T(8,128)(2,1)S(1)}, u32[]{:S(2)}, u32[]{:S(2)}) %collective-permute-start.11) | collective-permute-done | bytes 524320 | tf_op jit(solution)/shard_map/ppermute | solution.py:185
  69.2 0.0 copy-done.2
  69.2 0.0 copy-done.3
  69.2 0.0 copy-done.4
  69.2 3.0 %shard_map.92 = bf16[2,256,512]{2,1,0:T(8,128)(2,1)} custom-call(s32[3]{0:T(128)S(1)} %pad_add_fusion.pos_ref, f32[4]{0:T(128)S(1)} %copy-done.3, s32[4]{0:T(128)S(1)} %copy-done.4, bf16[2,256,512]{2,1,0:T(8,128)(2,1)S(1)} %shard_map.91.own_ref, bf16[2,256,512]{2,1,0:T(8,128)(2,1)S(1)} %collective-permute-done.11.b_ref, ...), custom_call_target="tpu_custom_call" | custom-call | flops 1073741824 | bytes 3145728 | tf_op jit(solution)/shard_map/pallas_call | solution.py:140
  72.1 6.4 %collective-permute-done.9.a_ref = bf16[2,256,512]{2,1,0:T(8,128)(2,1)S(1)} collective-permute-done((bf16[2,256,512]{2,1,0:T(8,128)(2,1)S(1)}, bf16[2,256,512]{2,1,0:T(8,128)(2,1)S(1)}, u32[]{:S(2)}, u32[]{:S(2)}) %collective-permute-start.9) | collective-permute-done | bytes 524320 | tf_op jit(solution)/shard_map/ppermute | solution.py:184
  78.5 1.1 %collective-permute-done.8.b_ref = bf16[2,256,512]{2,1,0:T(8,128)(2,1)S(1)} collective-permute-done((bf16[2,256,512]{2,1,0:T(8,128)(2,1)S(1)}, bf16[2,256,512]{2,1,0:T(8,128)(2,1)S(1)}, u32[]{:S(2)}, u32[]{:S(2)}) %collective-permute-start.8) | collective-permute-done | bytes 524320 | tf_op jit(solution)/shard_map/ppermute | solution.py:183
  79.7 3.0 %shard_map.90 = bf16[2,256,512]{2,1,0:T(8,128)(2,1)} custom-call(s32[3]{0:T(128)S(1)} %pad_add_fusion.pos_ref, f32[4]{0:T(128)S(1)} %copy-done.3, s32[4]{0:T(128)S(1)} %copy-done.4, bf16[2,256,512]{2,1,0:T(8,128)(2,1)S(1)} %shard_map.89.own_ref, bf16[2,256,512]{2,1,0:T(8,128)(2,1)S(1)} %collective-permute-done.8.b_ref, ...), custom_call_target="tpu_custom_call" | custom-call | flops 1073741824 | bytes 3145728 | tf_op jit(solution)/shard_map/pallas_call | solution.py:140
  (1 shorter events, 0.0 us)
Async XLA Ops:
  0.6 15.4 %copy-start.5 = (f32[5]{0:T(128)S(1)}, f32[5]{0:T(128)}, u32[]{:S(2)}) copy-start(f32[5]{0:T(128)} %param.13) | copy-start | bytes 64
  0.6 15.4 %copy-start.6 = (s32[1,5]{1,0:T(1,128)S(1)}, s32[1,5]{1,0:T(1,128)}, u32[]{:S(2)}) copy-start(s32[1,5]{1,0:T(1,128)} %param.12) | copy-start | bytes 64
  0.6 23.0 %collective-permute-start.3 = (bf16[2,256,512]{2,1,0:T(8,128)(2,1)}, bf16[2,256,512]{2,1,0:T(8,128)(2,1)S(1)}, u32[]{:S(2)}, u32[]{:S(2)}) collective-permute-start(bf16[2,256,512]{2,1,0:T(8,128)(2,1)} %bitcast.16), channel_id=1, source_target_pairs={{0,480},{8,488},{16,48},{24,56},{32,0},{40,8},{48,80},{56,88},{64,... | collective-permute-start | bytes 1572872 | tf_op jit(solution)/shard_map/ppermute | solution.py:157
  12.2 15.6 %collective-permute-start = (bf16[2,256,512]{2,1,0:T(8,128)(2,1)}, bf16[2,256,512]{2,1,0:T(8,128)(2,1)S(1)}, u32[]{:S(2)}, u32[]{:S(2)}) collective-permute-start(bf16[2,256,512]{2,1,0:T(8,128)(2,1)} %bitcast.14), channel_id=1, source_target_pairs={{0,16},{8,24},{16,0},{24,8},{32,48},{40,56},{48,32},{56,40},{64,80... | collective-permute-start | bytes 1572872 | tf_op jit(solution)/shard_map/ppermute | solution.py:157
  14.1 15.6 %collective-permute-start.4 = (bf16[2,256,512]{2,1,0:T(8,128)(2,1)}, bf16[2,256,512]{2,1,0:T(8,128)(2,1)S(1)}, u32[]{:S(2)}, u32[]{:S(2)}) collective-permute-start(bf16[2,256,512]{2,1,0:T(8,128)(2,1)} %bitcast.17), channel_id=1, source_target_pairs={{0,8},{8,0},{16,24},{24,16},{32,40},{40,32},{48,56},{56,48},{64,72... | collective-permute-start | bytes 1572872 | tf_op jit(solution)/shard_map/ppermute | solution.py:157
  16.1 11.7 %collective-permute-start.1 = (f32[5]{0:T(128)S(1)}, f32[5]{0:T(128)S(1)}, u32[]{:S(2)}, u32[]{:S(2)}) collective-permute-start(f32[5]{0:T(128)S(1)} %bitcast_multiply_fusion.f_ref), channel_id=1, source_target_pairs={{0,16},{8,24},{16,0},{24,8},{32,48},{40,56},{48,32},{56,40},{64,80... | collective-permute-start | bytes 68 | tf_op jit(solution)/shard_map/ppermute | solution.py:157
  20.0 1.0 %copy-start = (bf16[1,2,1,256,512]{4,3,2,1,0:T(8,128)(2,1)S(1)}, bf16[1,2,1,256,512]{4,3,2,1,0:T(8,128)(2,1)}, u32[]{:S(2)}) copy-start(bf16[1,2,1,256,512]{4,3,2,1,0:T(8,128)(2,1)} %param.7) | copy-start | bytes 1572868
  21.1 1.0 %copy-start.1 = (bf16[1,2,1,256,512]{4,3,2,1,0:T(8,128)(2,1)S(1)}, bf16[1,2,1,256,512]{4,3,2,1,0:T(8,128)(2,1)}, u32[]{:S(2)}) copy-start(bf16[1,2,1,256,512]{4,3,2,1,0:T(8,128)(2,1)} %param.8) | copy-start | bytes 1572868
  23.7 6.0 %collective-permute-start.5 = (bf16[2,256,512]{2,1,0:T(8,128)(2,1)S(1)}, bf16[2,256,512]{2,1,0:T(8,128)(2,1)S(1)}, u32[]{:S(2)}, u32[]{:S(2)}) collective-permute-start(bf16[2,256,512]{2,1,0:T(8,128)(2,1)S(1)} %collective-permute-done.3.z_ref), channel_id=1, source_target_pairs={{0,8},{8,0},{16,24},{24,16},{32,40},{40,32},{48,56},{56,48},{64,72... | collective-permute-start | bytes 1572872 | tf_op jit(solution)/shard_map/ppermute | solution.py:157
  27.8 16.0 %collective-permute-start.2 = (bf16[2,256,512]{2,1,0:T(8,128)(2,1)S(1)}, bf16[2,256,512]{2,1,0:T(8,128)(2,1)S(1)}, u32[]{:S(2)}, u32[]{:S(2)}) collective-permute-start(bf16[2,256,512]{2,1,0:T(8,128)(2,1)S(1)} %collective-permute-done.y_ref), channel_id=1, source_target_pairs={{0,32},{8,40},{16,496},{24,504},{32,64},{40,72},{48,16},{56,24},{6... | collective-permute-start | bytes 1572872 | tf_op jit(solution)/shard_map/ppermute | solution.py:157
  30.6 16.1 %collective-permute-start.10 = (bf16[2,256,512]{2,1,0:T(8,128)(2,1)S(1)}, bf16[2,256,512]{2,1,0:T(8,128)(2,1)S(1)}, u32[]{:S(2)}, u32[]{:S(2)}) collective-permute-start(bf16[2,256,512]{2,1,0:T(8,128)(2,1)S(1)} %shard_map.87), channel_id=1, source_target_pairs={{0,16},{8,24},{16,0},{24,8},{32,48},{40,56},{48,32},{56,40},{64,80... | collective-permute-start | bytes 1572872 | tf_op jit(solution)/shard_map/ppermute | solution.py:157
  34.4 9.3 %collective-permute-start.6 = (f32[5]{0:T(128)S(1)}, f32[5]{0:T(128)S(1)}, u32[]{:S(2)}, u32[]{:S(2)}) collective-permute-start(f32[5]{0:T(128)S(1)} %bitcast_multiply_fusion.f_ref), channel_id=1, source_target_pairs={{0,8},{8,0},{16,24},{24,16},{32,40},{40,32},{48,56},{56,48},{64,72... | collective-permute-start | bytes 68 | tf_op jit(solution)/shard_map/ppermute | solution.py:157
  44.6 9.8 %collective-permute-start.7 = (bf16[2,256,512]{2,1,0:T(8,128)(2,1)S(1)}, bf16[2,256,512]{2,1,0:T(8,128)(2,1)S(1)}, u32[]{:S(2)}, u32[]{:S(2)}) collective-permute-start(bf16[2,256,512]{2,1,0:T(8,128)(2,1)S(1)} %shard_map.88), channel_id=1, source_target_pairs={{0,8},{8,0},{16,24},{24,16},{32,40},{40,32},{48,56},{56,48},{64,72... | collective-permute-start | bytes 1572872 | tf_op jit(solution)/shard_map/ppermute | solution.py:157
  47.5 21.6 %copy-start.2 = (bf16[1,4,256,256]{3,2,1,0:T(8,128)(2,1)S(1)}, bf16[1,4,256,256]{3,2,1,0:T(8,128)(2,1)}, u32[]{:S(2)}) copy-start(bf16[1,4,256,256]{3,2,1,0:T(8,128)(2,1)} %param.9) | copy-start | bytes 1572868
  47.5 20.4 %collective-permute-start.12 = (bf16[2,256,512]{2,1,0:T(8,128)(2,1)S(1)}, bf16[2,256,512]{2,1,0:T(8,128)(2,1)S(1)}, u32[]{:S(2)}, u32[]{:S(2)}) collective-permute-start(bf16[2,256,512]{2,1,0:T(8,128)(2,1)S(1)} %shard_map.91.own_ref), channel_id=1, source_target_pairs={{1,2},{3,4},{5,6},{2,1},{4,3},{6,5},{9,10},{11,12},{13,14},{10,9},... | collective-permute-start | bytes 1572872 | tf_op jit(solution)/shard_map/ppermute | solution.py:186
  52.5 16.7 %collective-permute-start.11 = (bf16[2,256,512]{2,1,0:T(8,128)(2,1)S(1)}, bf16[2,256,512]{2,1,0:T(8,128)(2,1)S(1)}, u32[]{:S(2)}, u32[]{:S(2)}) collective-permute-start(bf16[2,256,512]{2,1,0:T(8,128)(2,1)S(1)} %shard_map.91.own_ref), channel_id=1, source_target_pairs={{0,1},{2,3},{4,5},{6,7},{1,0},{3,2},{5,4},{7,6},{8,9},{10,11},{12,... | collective-permute-start | bytes 1572872 | tf_op jit(solution)/shard_map/ppermute | solution.py:185
  55.4 13.8 %copy-start.3 = (f32[4]{0:T(128)S(1)}, f32[4]{0:T(128)}, u32[]{:S(2)}) copy-start(f32[4]{0:T(128)} %occ_ref.3) | copy-start | bytes 52
  55.4 13.8 %copy-start.4 = (s32[4]{0:T(128)S(1)}, s32[4]{0:T(128)}, u32[]{:S(2)}) copy-start(s32[4]{0:T(128)} %off_ref.3) | copy-start | bytes 52
  55.4 23.2 %collective-permute-start.9 = (bf16[2,256,512]{2,1,0:T(8,128)(2,1)S(1)}, bf16[2,256,512]{2,1,0:T(8,128)(2,1)S(1)}, u32[]{:S(2)}, u32[]{:S(2)}) collective-permute-start(bf16[2,256,512]{2,1,0:T(8,128)(2,1)S(1)} %shard_map.89.own_ref), channel_id=1, source_target_pairs={{1,2},{3,4},{5,6},{2,1},{4,3},{6,5},{9,10},{11,12},{13,14},{10,9},... | collective-permute-start | bytes 1572872 | tf_op jit(solution)/shard_map/ppermute | solution.py:184
  60.3 19.4 %collective-permute-start.8 = (bf16[2,256,512]{2,1,0:T(8,128)(2,1)S(1)}, bf16[2,256,512]{2,1,0:T(8,128)(2,1)S(1)}, u32[]{:S(2)}, u32[]{:S(2)}) collective-permute-start(bf16[2,256,512]{2,1,0:T(8,128)(2,1)S(1)} %shard_map.89.own_ref), channel_id=1, source_target_pairs={{0,1},{2,3},{4,5},{6,7},{1,0},{3,2},{5,4},{7,6},{8,9},{10,11},{12,... | collective-permute-start | bytes 1572872 | tf_op jit(solution)/shard_map/ppermute | solution.py:183

commit v4 on v3

--- a/solution.py
+++ b/solution.py
@@ -68,19 +68,33 @@
     weighted((f_ref[2], jnp.where(core1, f_ref[3], f_ref[1]), None), (x_ref, c_ref, r_ref), out_ref)
 
 
-def lesser_window_kernel(pos_ref, f_ref, x_ref, y_ref, z_ref, r_ref, out_ref):
+def lesser_window_kernel(pos_ref, f_ref, w_ref, x_ref, y_ref, z_ref, r_ref, first_ref, last_ref):
     odd = pos_ref[1] == 1
+    f = f_ref[2]
     fy = jnp.where(odd, f_ref[4], f_ref[0])
     fz = jnp.where(odd, f_ref[0], f_ref[4])
-    weighted((f_ref[2], fy, fz, None), (x_ref, y_ref, z_ref, r_ref), out_ref)
-
-
-def combine(kernel, pos, factors, *blocks):
+    for e in range(2):
+        for r in range(0, ORB, ROWS):
+            rows = slice(r, r + ROWS)
+            first_ref[e, rows, : 2 * ORB] = w_ref[e, rows, :]
+            w = (
+                f * x_ref[e, rows, :].astype(F32)
+                + fy * y_ref[e, rows, :].astype(F32)
+                + fz * z_ref[e, rows, :].astype(F32)
+                + r_ref[e, rows, :].astype(F32)
+            ).astype(BF16)
+            first_ref[e, rows, 2 * ORB :] = w[:, :ORB]
+            last_ref[e, rows, :] = w[:, ORB:]
+
+
+def combine(kernel, pos, factors, *blocks, widths=None):
+    single = widths is None
+    shapes = [jax.ShapeDtypeStruct((2, ORB, w), BF16) for w in (widths or (2 * ORB,))]
     return pl.pallas_call(
         kernel,
-        out_shape=jax.ShapeDtypeStruct(SHAPE, BF16),
+        out_shape=shapes[0] if single else shapes,
         in_specs=[SMEM, SMEM] + [VMEM] * len(blocks),
-        out_specs=VMEM,
+        out_specs=VMEM if single else [VMEM] * len(shapes),
         compiler_params=PARAMS,
         cost_estimate=pl.CostEstimate(flops=2**21, bytes_accessed=2**21, transcendentals=0),
     )(pos, factors, *blocks)
@@ -124,24 +138,37 @@
     pl.when(jnp.logical_not(swap))(lambda: body(a_ref, b_ref))
 
 
-def sigma_kernel(pos_ref, occ_ref, off_ref, own_ref, b_ref, a_ref, mat_ref, out_ref, *, plus_up):
+def first_sigma_kernel(pos_ref, occ_ref, off_ref, own_ref, b_ref, a_ref, mat_ref, greater_ref, real_ref):
     def body(below_ref, above_ref):
         for e in range(2):
-            for h in range(2):
+            for h in range(3):
                 cols = slice(h * ORB, (h + 1) * ORB)
-                out_ref[e, :, cols] = sigma_part(
-                    occ_ref, off_ref, own_ref, below_ref, above_ref, mat_ref, e, cols, plus_up
-                )
+                part = sigma_part(occ_ref, off_ref, own_ref, below_ref, above_ref, mat_ref, e, cols, h == 2)
+                if h < 2:
+                    greater_ref[e, :, cols] = part
+                else:
+                    real_ref[e] = part
 
     by_parity(pos_ref, a_ref, b_ref, body)
 
 
-def sigma(plus_up, pos, occupation, offsets, *blocks):
+def last_sigma_kernel(pos_ref, occ_ref, off_ref, own_ref, b_ref, a_ref, mat_ref, real_ref, lesser_ref):
+    lesser_ref[:, :, :ORB] = real_ref[...]
+
+    def body(below_ref, above_ref):
+        for e in range(2):
+            part = sigma_part(occ_ref, off_ref, own_ref, below_ref, above_ref, mat_ref, e, slice(0, ORB), True)
+            lesser_ref[e, :, ORB:] = part
+
+    by_parity(pos_ref, a_ref, b_ref, body)
+
+
+def sigma(kernel, widths, pos, occupation, offsets, *blocks):
     return pl.pallas_call(
-        functools.partial(sigma_kernel, plus_up=plus_up),
-        out_shape=jax.ShapeDtypeStruct(SHAPE, BF16),
+        kernel,
+        out_shape=[jax.ShapeDtypeStruct((2, ORB, w), BF16) for w in widths],
         in_specs=[SMEM] * 3 + [VMEM] * len(blocks),
-        out_specs=VMEM,
+        out_specs=[VMEM] * len(widths),
         compiler_params=PARAMS,
         cost_estimate=pl.CostEstimate(flops=2**30, bytes_accessed=3 * 2**20, transcendentals=0),
     )(pos, occupation, offsets, *blocks)
@@ -177,15 +204,16 @@
     ql = combine(core_partial_kernel, pos, fc, xlv, yl, zl)
     rl = kz(ql, swap_route(count, 1))
     wg = combine(greater_window_kernel, pos, f, xgv, cg, rg)
-    wl = combine(lesser_window_kernel, pos, f, xlv, yl, zl, rl)
+    w1, w2 = combine(lesser_window_kernel, pos, f, wg, xlv, yl, zl, rl, widths=(3 * ORB, ORB))
 
     odd_pairs, even_pairs = pair_route(energies, 1), pair_route(energies, 0)
-    bl = lax.ppermute(wl, "en", even_pairs)
-    al = lax.ppermute(wl, "en", odd_pairs)
-    bg = lax.ppermute(wg, "en", even_pairs)
-    ag = lax.ppermute(wg, "en", odd_pairs)
-    sl = sigma(True, pos, occupation, offsets, wl, bl, al, mats)
-    sg = sigma(False, pos, occupation, offsets, wg, bg, ag, mats)
+    b1 = lax.ppermute(w1, "en", even_pairs)
+    a1 = lax.ppermute(w1, "en", odd_pairs)
+    a2 = lax.ppermute(w2, "en", odd_pairs)
+    b2 = lax.ppermute(w2, "en", even_pairs)
+    sg, real = sigma(first_sigma_kernel, (2 * ORB, ORB), pos, occupation, offsets, w1, b1, a1, mats)
+    a2, b2, sg, real = lax.optimization_barrier((a2, b2, sg, real))
+    (sl,) = sigma(last_sigma_kernel, (2 * ORB,), pos, occupation, offsets, w2, b2, a2, mats, real)
     return sl.reshape(lesser.shape), sg.reshape(greater.shape)
 
 

time: 83.2 us -> 86.2 us (1.036)
  starting transfers between devices: 44.4 us -> 48.1 us
    ppermute x9, starting transfers between devices: 30.7 us -> 32.8 us  [kz(): return lax.ppermute(block, 'kz', route)]
    ppermute x4, waiting for transfers between devices: 14.5 us -> 12.8 us  [the longest x1 10.5 us: local(): a1 = lax.ppermute(w1, 'en', odd_pairs)]
    ppermute x4, starting transfers between devices: 13.7 us -> 15.3 us  [the longest x1 5.02 us: local(): a1 = lax.ppermute(w1, 'en', odd_pairs)]
    ppermute x9, waiting for transfers between devices: 11.2 us -> 12.1 us  [kz(): return lax.ppermute(block, 'kz', route)]
  transfers between devices with their start and end apart: 13 -> 13, of which waited for: 8 -> 7; matrix products, arithmetic and copies ran while one was open for 0% -> 0% of each run, Pallas kernels for 8% -> 7%
where the time goes in v4:
time: 86.2 us; the launch traced here: 85.7 us
  starting transfers between devices  48.1 us (56%)
  waiting for transfers between devices  24.9 us (29%)
  Pallas kernels  9.66 us (11%)
  local copies, waits for them, and re-layouts  2.11 us (2%)
  between operations  0.87 us (1%)
    ppermute x9, starting transfers between devices, kz(): return lax.ppermute(block, 'kz', route)  32.8 us
    ppermute x9, waiting for transfers between devices, kz(): return lax.ppermute(block, 'kz', route)  12.1 us
    ppermute x1, waiting for transfers between devices, local(): a1 = lax.ppermute(w1, 'en', odd_pairs)  10.5 us
    pallas_call x2, Pallas kernels, sigma(): pl.pallas_call(kernel, out_shape=[jax.ShapeDtypeStruct((2, ORB, w), BF16)...  6.09 us
    ppermute x1, starting transfers between devices, local(): a1 = lax.ppermute(w1, 'en', odd_pairs)  5.02 us
    ppermute x1, starting transfers between devices, local(): a2 = lax.ppermute(w2, 'en', odd_pairs)  4.44 us
    ppermute x1, starting transfers between devices, local(): b2 = lax.ppermute(w2, 'en', even_pairs)  3.92 us
    pallas_call x4, Pallas kernels, combine(): pl.pallas_call(kernel, out_shape=shapes[0] if single else shapes, in_spec...  3.5 us
  transfers between devices with their start and end apart: 13, of which 7 were waited for; matrix products, arithmetic and copies ran while one was open for 0% of the time, Pallas kernels for 7%

profile of v4, /device:TPU:6, one launch (start us, length us, event | category | flops | bytes accessed | tf_op | source)
XLA Modules:
  0.0 85.7 jit_solution(13679483204767775503)
XLA Ops:
  0.6 0.0 copy-start.5
  0.6 0.0 copy-start.6
  0.6 11.5 %collective-permute-start.3 = (bf16[2,256,512]{2,1,0:T(8,128)(2,1)}, bf16[2,256,512]{2,1,0:T(8,128)(2,1)S(1)}, u32[]{:S(2)}, u32[]{:S(2)}) collective-permute-start(bf16[2,256,512]{2,1,0:T(8,128)(2,1)} %bitcast.16), channel_id=1, source_target_pairs={{0,480},{8,488},{16,48},{24,56},{32,0},{40,8},{48,80},{56,88},{64,... | collective-permute-start | bytes 1572872 | tf_op jit(solution)/shard_map/ppermute | solution.py:184
  12.2 1.9 %collective-permute-start = (bf16[2,256,512]{2,1,0:T(8,128)(2,1)}, bf16[2,256,512]{2,1,0:T(8,128)(2,1)S(1)}, u32[]{:S(2)}, u32[]{:S(2)}) collective-permute-start(bf16[2,256,512]{2,1,0:T(8,128)(2,1)} %bitcast.14), channel_id=1, source_target_pairs={{0,16},{8,24},{16,0},{24,8},{32,48},{40,56},{48,32},{56,40},{64,80... | collective-permute-start | bytes 1572872 | tf_op jit(solution)/shard_map/ppermute | solution.py:184
  14.1 1.9 %collective-permute-start.2 = (bf16[2,256,512]{2,1,0:T(8,128)(2,1)}, bf16[2,256,512]{2,1,0:T(8,128)(2,1)S(1)}, u32[]{:S(2)}, u32[]{:S(2)}) collective-permute-start(bf16[2,256,512]{2,1,0:T(8,128)(2,1)} %bitcast.17), channel_id=1, source_target_pairs={{0,8},{8,0},{16,24},{24,16},{32,40},{40,32},{48,56},{56,48},{64,72... | collective-permute-start | bytes 1572872 | tf_op jit(solution)/shard_map/ppermute | solution.py:184
  16.1 0.0 copy-done.5
  16.1 0.0 copy-done.6
  16.1 3.9 %collective-permute-start.1 = (f32[5]{0:T(128)S(1)}, f32[5]{0:T(128)S(1)}, u32[]{:S(2)}, u32[]{:S(2)}) collective-permute-start(f32[5]{0:T(128)S(1)} %bitcast_multiply_fusion.f_ref), channel_id=1, source_target_pairs={{0,16},{8,24},{16,0},{24,8},{32,48},{40,56},{48,32},{56,40},{64,80... | collective-permute-start | bytes 68 | tf_op jit(solution)/shard_map/ppermute | solution.py:184
  20.0 3.6 %collective-permute-done.3.z_ref = bf16[2,256,512]{2,1,0:T(8,128)(2,1)S(1)} collective-permute-done((bf16[2,256,512]{2,1,0:T(8,128)(2,1)}, bf16[2,256,512]{2,1,0:T(8,128)(2,1)S(1)}, u32[]{:S(2)}, u32[]{:S(2)}) %collective-permute-start.3) | collective-permute-done | bytes 524320 | tf_op jit(solution)/shard_map/ppermute | solution.py:184
  23.7 1.9 %collective-permute-start.4 = (bf16[2,256,512]{2,1,0:T(8,128)(2,1)S(1)}, bf16[2,256,512]{2,1,0:T(8,128)(2,1)S(1)}, u32[]{:S(2)}, u32[]{:S(2)}) collective-permute-start(bf16[2,256,512]{2,1,0:T(8,128)(2,1)S(1)} %collective-permute-done.3.z_ref), channel_id=1, source_target_pairs={{0,8},{8,0},{16,24},{24,16},{32,40},{40,32},{48,56},{56,48},{64,72... | collective-permute-start | bytes 1572872 | tf_op jit(solution)/shard_map/ppermute | solution.py:184
  25.6 0.1 pad_add_fusion.pos_ref
  25.7 0.0 copy-start
  25.7 1.0 %copy-done = bf16[1,2,1,256,512]{4,3,2,1,0:T(8,128)(2,1)S(1)} copy-done((bf16[1,2,1,256,512]{4,3,2,1,0:T(8,128)(2,1)S(1)}, bf16[1,2,1,256,512]{4,3,2,1,0:T(8,128)(2,1)}, u32[]{:S(2)}) %copy-start) | copy-done | bytes 524312
  26.7 0.0 copy-start.1
  26.7 1.0 %copy-done.1 = bf16[1,2,1,256,512]{4,3,2,1,0:T(8,128)(2,1)S(1)} copy-done((bf16[1,2,1,256,512]{4,3,2,1,0:T(8,128)(2,1)S(1)}, bf16[1,2,1,256,512]{4,3,2,1,0:T(8,128)(2,1)}, u32[]{:S(2)}) %copy-start.1) | copy-done | bytes 524312
  27.7 0.1 shard_map.86
  27.8 0.0 collective-permute-done.1.f_ref
  27.8 0.0 collective-permute-done.y_ref
  27.8 1.9 %collective-permute-start.6 = (bf16[2,256,512]{2,1,0:T(8,128)(2,1)S(1)}, bf16[2,256,512]{2,1,0:T(8,128)(2,1)S(1)}, u32[]{:S(2)}, u32[]{:S(2)}) collective-permute-start(bf16[2,256,512]{2,1,0:T(8,128)(2,1)S(1)} %collective-permute-done.y_ref), channel_id=1, source_target_pairs={{0,32},{8,40},{16,496},{24,504},{32,64},{40,72},{48,16},{56,24},{6... | collective-permute-start | bytes 1572872 | tf_op jit(solution)/shard_map/ppermute | solution.py:184
  29.8 0.0 collective-permute-done.2.c_ref
  29.8 0.0 collective-permute-done.4.cz_ref
  29.8 0.9 %shard_map.87 = bf16[2,256,512]{2,1,0:T(8,128)(2,1)S(1)} custom-call(s32[3]{0:T(128)S(1)} %pad_add_fusion.pos_ref, f32[5]{0:T(128)S(1)} %collective-permute-done.1.f_ref, bf16[2,256,512]{2,1,0:T(8,128)(2,1)S(1)} %get-tuple-element.25.x_ref, bf16[2,256,512]{2,1,0:T(8,128)(2,1)S(1)} %collective-permute-done.3.z_ref, ...), custom_call_target="tpu_custom_call" | custom-call | flops 2097152 | bytes 2097152 | tf_op jit(solution)/shard_map/pallas_call | solution.py:93
  30.7 5.8 %collective-permute-start.5 = (bf16[2,256,512]{2,1,0:T(8,128)(2,1)S(1)}, bf16[2,256,512]{2,1,0:T(8,128)(2,1)S(1)}, u32[]{:S(2)}, u32[]{:S(2)}) collective-permute-start(bf16[2,256,512]{2,1,0:T(8,128)(2,1)S(1)} %shard_map.87), channel_id=1, source_target_pairs={{0,16},{8,24},{16,0},{24,8},{32,48},{40,56},{48,32},{56,40},{64,80... | collective-permute-start | bytes 1572872 | tf_op jit(solution)/shard_map/ppermute | solution.py:184
  36.6 1.9 %collective-permute-start.7 = (f32[5]{0:T(128)S(1)}, f32[5]{0:T(128)S(1)}, u32[]{:S(2)}, u32[]{:S(2)}) collective-permute-start(f32[5]{0:T(128)S(1)} %bitcast_multiply_fusion.f_ref), channel_id=1, source_target_pairs={{0,8},{8,0},{16,24},{24,16},{32,40},{40,32},{48,56},{56,48},{64,72... | collective-permute-start | bytes 68 | tf_op jit(solution)/shard_map/ppermute | solution.py:184
  38.5 7.4 %collective-permute-done.6.z_ref = bf16[2,256,512]{2,1,0:T(8,128)(2,1)S(1)} collective-permute-done((bf16[2,256,512]{2,1,0:T(8,128)(2,1)S(1)}, bf16[2,256,512]{2,1,0:T(8,128)(2,1)S(1)}, u32[]{:S(2)}, u32[]{:S(2)}) %collective-permute-start.6) | collective-permute-done | bytes 524320 | tf_op jit(solution)/shard_map/ppermute | solution.py:184
  45.9 0.0 collective-permute-done.7.f_ref
  45.9 0.8 shard_map.89
  46.8 1.9 %collective-permute-start.8 = (bf16[2,256,512]{2,1,0:T(8,128)(2,1)S(1)}, bf16[2,256,512]{2,1,0:T(8,128)(2,1)S(1)}, u32[]{:S(2)}, u32[]{:S(2)}) collective-permute-start(bf16[2,256,512]{2,1,0:T(8,128)(2,1)S(1)} %shard_map.89), channel_id=1, source_target_pairs={{0,8},{8,0},{16,24},{24,16},{32,40},{40,32},{48,56},{56,48},{64,72... | collective-permute-start | bytes 1572872 | tf_op jit(solution)/shard_map/ppermute | solution.py:184
  48.7 0.2 collective-permute-done.5.r_ref
  48.9 0.8 shard_map.88.w_ref
  49.7 0.0 copy-start.2
  49.7 0.9 %collective-permute-done.8.r_ref = bf16[2,256,512]{2,1,0:T(8,128)(2,1)S(1)} collective-permute-done((bf16[2,256,512]{2,1,0:T(8,128)(2,1)S(1)}, bf16[2,256,512]{2,1,0:T(8,128)(2,1)S(1)}, u32[]{:S(2)}, u32[]{:S(2)}) %collective-permute-start.8) | collective-permute-done | bytes 524320 | tf_op jit(solution)/shard_map/ppermute | solution.py:184
  50.6 0.9 %shard_map.90 = (bf16[2,256,768]{2,1,0:T(8,128)(2,1)S(1)}, bf16[2,256,256]{2,1,0:T(8,128)(2,1)S(1)}) custom-call(s32[3]{0:T(128)S(1)} %pad_add_fusion.pos_ref, f32[5]{0:T(128)S(1)} %bitcast_multiply_fusion.f_ref, bf16[2,256,512]{2,1,0:T(8,128)(2,1)S(1)} %shard_map.88.w_ref, bf16[2,256,512]{2,1,0:T(8,128)(2,1)S(1)} %get-tuple-element.27.x_ref, ...), custom_call_target="tpu_custom_call" | custom-call | flops 2097152 | bytes 2097152 | tf_op jit(solution)/shard_map/pallas_call | solution.py:93
  51.5 5.0 %collective-permute-start.12 = (bf16[2,256,768]{2,1,0:T(8,128)(2,1)S(1)}, bf16[2,256,768]{2,1,0:T(8,128)(2,1)S(1)}, u32[]{:S(2)}, u32[]{:S(2)}) collective-permute-start(bf16[2,256,768]{2,1,0:T(8,128)(2,1)S(1)} %get-tuple-element.33.own_ref), channel_id=1, source_target_pairs={{1,2},{3,4},{5,6},{2,1},{4,3},{6,5},{9,10},{11,12},{13,14},{10,9},... | collective-permute-start | bytes 2359304 | tf_op jit(solution)/shard_map/ppermute | solution.py:211
  56.5 1.9 %collective-permute-start.11 = (bf16[2,256,768]{2,1,0:T(8,128)(2,1)S(1)}, bf16[2,256,768]{2,1,0:T(8,128)(2,1)S(1)}, u32[]{:S(2)}, u32[]{:S(2)}) collective-permute-start(bf16[2,256,768]{2,1,0:T(8,128)(2,1)S(1)} %get-tuple-element.33.own_ref), channel_id=1, source_target_pairs={{0,1},{2,3},{4,5},{6,7},{1,0},{3,2},{5,4},{7,6},{8,9},{10,11},{12,... | collective-permute-start | bytes 2359304 | tf_op jit(solution)/shard_map/ppermute | solution.py:210
  58.4 0.0 copy-start.3
  58.5 0.0 copy-start.4
  58.5 3.9 %collective-permute-start.10 = (bf16[2,256,256]{2,1,0:T(8,128)(2,1)S(1)}, bf16[2,256,256]{2,1,0:T(8,128)(2,1)S(1)}, u32[]{:S(2)}, u32[]{:S(2)}) collective-permute-start(bf16[2,256,256]{2,1,0:T(8,128)(2,1)S(1)} %get-tuple-element.32.own_ref), channel_id=1, source_target_pairs={{0,1},{2,3},{4,5},{6,7},{1,0},{3,2},{5,4},{7,6},{8,9},{10,11},{12,... | collective-permute-start | bytes 786440 | tf_op jit(solution)/shard_map/ppermute | solution.py:213
  62.4 4.4 %collective-permute-start.9 = (bf16[2,256,256]{2,1,0:T(8,128)(2,1)S(1)}, bf16[2,256,256]{2,1,0:T(8,128)(2,1)S(1)}, u32[]{:S(2)}, u32[]{:S(2)}) collective-permute-start(bf16[2,256,256]{2,1,0:T(8,128)(2,1)S(1)} %get-tuple-element.32.own_ref), channel_id=1, source_target_pairs={{1,2},{3,4},{5,6},{2,1},{4,3},{6,5},{9,10},{11,12},{13,14},{10,9},... | collective-permute-start | bytes 786440 | tf_op jit(solution)/shard_map/ppermute | solution.py:212
  66.8 10.5 %collective-permute-done.12.a_ref = bf16[2,256,768]{2,1,0:T(8,128)(2,1)S(1)} collective-permute-done((bf16[2,256,768]{2,1,0:T(8,128)(2,1)S(1)}, bf16[2,256,768]{2,1,0:T(8,128)(2,1)S(1)}, u32[]{:S(2)}, u32[]{:S(2)}) %collective-permute-start.12) | collective-permute-done | bytes 786464 | tf_op jit(solution)/shard_map/ppermute | solution.py:211
  77.4 1.5 %collective-permute-done.11.b_ref = bf16[2,256,768]{2,1,0:T(8,128)(2,1)S(1)} collective-permute-done((bf16[2,256,768]{2,1,0:T(8,128)(2,1)S(1)}, bf16[2,256,768]{2,1,0:T(8,128)(2,1)S(1)}, u32[]{:S(2)}, u32[]{:S(2)}) %collective-permute-start.11) | collective-permute-done | bytes 786464 | tf_op jit(solution)/shard_map/ppermute | solution.py:210
  78.8 0.0 copy-done.2
  78.8 0.0 copy-done.3
  78.8 0.0 copy-done.4
  78.9 3.7 %shard_map.91 = (bf16[2,256,512]{2,1,0:T(8,128)(2,1)}, bf16[2,256,256]{2,1,0:T(8,128)(2,1)S(1)}) custom-call(s32[3]{0:T(128)S(1)} %pad_add_fusion.pos_ref, f32[4]{0:T(128)S(1)} %copy-done.3, s32[4]{0:T(128)S(1)} %copy-done.4, bf16[2,256,768]{2,1,0:T(8,128)(2,1)S(1)} %get-tuple-element.33.own_ref, bf16[2,256,768]{2,1,0:T(8,128)(2,1)S(1)} %collective-permute-done.11.b_ref, ...), custom_call_target="tpu_custom_call" | custom-call | flops 1073741824 | bytes 3145728 | tf_op jit(solution)/shard_map/pallas_call | solution.py:167
  82.6 0.8 collective-permute-done.10.b_ref
  83.3 0.0 collective-permute-done.9.a_ref
  83.3 2.4 %shard_map.92 = bf16[2,256,512]{2,1,0:T(8,128)(2,1)} custom-call(s32[3]{0:T(128)S(1)} %pad_add_fusion.pos_ref, f32[4]{0:T(128)S(1)} %copy-done.3, s32[4]{0:T(128)S(1)} %copy-done.4, bf16[2,256,256]{2,1,0:T(8,128)(2,1)S(1)} %get-tuple-element.32.own_ref, bf16[2,256,256]{2,1,0:T(8,128)(2,1)S(1)} %collective-permute-done.10.b_ref, ...), custom_call_target="tpu_custom_call" | custom-call | flops 1073741824 | bytes 3145728 | tf_op jit(solution)/shard_map/pallas_call | solution.py:167
  (1 shorter events, 0.0 us)
Async XLA Ops:
  0.6 15.4 %copy-start.5 = (f32[5]{0:T(128)S(1)}, f32[5]{0:T(128)}, u32[]{:S(2)}) copy-start(f32[5]{0:T(128)} %param.13) | copy-start | bytes 64
  0.6 15.4 %copy-start.6 = (s32[1,5]{1,0:T(1,128)S(1)}, s32[1,5]{1,0:T(1,128)}, u32[]{:S(2)}) copy-start(s32[1,5]{1,0:T(1,128)} %param.12) | copy-start | bytes 64
  0.6 23.0 %collective-permute-start.3 = (bf16[2,256,512]{2,1,0:T(8,128)(2,1)}, bf16[2,256,512]{2,1,0:T(8,128)(2,1)S(1)}, u32[]{:S(2)}, u32[]{:S(2)}) collective-permute-start(bf16[2,256,512]{2,1,0:T(8,128)(2,1)} %bitcast.16), channel_id=1, source_target_pairs={{0,480},{8,488},{16,48},{24,56},{32,0},{40,8},{48,80},{56,88},{64,... | collective-permute-start | bytes 1572872 | tf_op jit(solution)/shard_map/ppermute | solution.py:184
  12.2 15.6 %collective-permute-start = (bf16[2,256,512]{2,1,0:T(8,128)(2,1)}, bf16[2,256,512]{2,1,0:T(8,128)(2,1)S(1)}, u32[]{:S(2)}, u32[]{:S(2)}) collective-permute-start(bf16[2,256,512]{2,1,0:T(8,128)(2,1)} %bitcast.14), channel_id=1, source_target_pairs={{0,16},{8,24},{16,0},{24,8},{32,48},{40,56},{48,32},{56,40},{64,80... | collective-permute-start | bytes 1572872 | tf_op jit(solution)/shard_map/ppermute | solution.py:184
  14.1 15.6 %collective-permute-start.2 = (bf16[2,256,512]{2,1,0:T(8,128)(2,1)}, bf16[2,256,512]{2,1,0:T(8,128)(2,1)S(1)}, u32[]{:S(2)}, u32[]{:S(2)}) collective-permute-start(bf16[2,256,512]{2,1,0:T(8,128)(2,1)} %bitcast.17), channel_id=1, source_target_pairs={{0,8},{8,0},{16,24},{24,16},{32,40},{40,32},{48,56},{56,48},{64,72... | collective-permute-start | bytes 1572872 | tf_op jit(solution)/shard_map/ppermute | solution.py:184
  16.1 11.7 %collective-permute-start.1 = (f32[5]{0:T(128)S(1)}, f32[5]{0:T(128)S(1)}, u32[]{:S(2)}, u32[]{:S(2)}) collective-permute-start(f32[5]{0:T(128)S(1)} %bitcast_multiply_fusion.f_ref), channel_id=1, source_target_pairs={{0,16},{8,24},{16,0},{24,8},{32,48},{40,56},{48,32},{56,40},{64,80... | collective-permute-start | bytes 68 | tf_op jit(solution)/shard_map/ppermute | solution.py:184
  23.7 6.1 %collective-permute-start.4 = (bf16[2,256,512]{2,1,0:T(8,128)(2,1)S(1)}, bf16[2,256,512]{2,1,0:T(8,128)(2,1)S(1)}, u32[]{:S(2)}, u32[]{:S(2)}) collective-permute-start(bf16[2,256,512]{2,1,0:T(8,128)(2,1)S(1)} %collective-permute-done.3.z_ref), channel_id=1, source_target_pairs={{0,8},{8,0},{16,24},{24,16},{32,40},{40,32},{48,56},{56,48},{64,72... | collective-permute-start | bytes 1572872 | tf_op jit(solution)/shard_map/ppermute | solution.py:184
  25.7 1.0 %copy-start = (bf16[1,2,1,256,512]{4,3,2,1,0:T(8,128)(2,1)S(1)}, bf16[1,2,1,256,512]{4,3,2,1,0:T(8,128)(2,1)}, u32[]{:S(2)}) copy-start(bf16[1,2,1,256,512]{4,3,2,1,0:T(8,128)(2,1)} %param.7) | copy-start | bytes 1572868
  26.7 1.0 %copy-start.1 = (bf16[1,2,1,256,512]{4,3,2,1,0:T(8,128)(2,1)S(1)}, bf16[1,2,1,256,512]{4,3,2,1,0:T(8,128)(2,1)}, u32[]{:S(2)}) copy-start(bf16[1,2,1,256,512]{4,3,2,1,0:T(8,128)(2,1)} %param.8) | copy-start | bytes 1572868
  27.8 18.1 %collective-permute-start.6 = (bf16[2,256,512]{2,1,0:T(8,128)(2,1)S(1)}, bf16[2,256,512]{2,1,0:T(8,128)(2,1)S(1)}, u32[]{:S(2)}, u32[]{:S(2)}) collective-permute-start(bf16[2,256,512]{2,1,0:T(8,128)(2,1)S(1)} %collective-permute-done.y_ref), channel_id=1, source_target_pairs={{0,32},{8,40},{16,496},{24,504},{32,64},{40,72},{48,16},{56,24},{6... | collective-permute-start | bytes 1572872 | tf_op jit(solution)/shard_map/ppermute | solution.py:184
  30.7 18.1 %collective-permute-start.5 = (bf16[2,256,512]{2,1,0:T(8,128)(2,1)S(1)}, bf16[2,256,512]{2,1,0:T(8,128)(2,1)S(1)}, u32[]{:S(2)}, u32[]{:S(2)}) collective-permute-start(bf16[2,256,512]{2,1,0:T(8,128)(2,1)S(1)} %shard_map.87), channel_id=1, source_target_pairs={{0,16},{8,24},{16,0},{24,8},{32,48},{40,56},{48,32},{56,40},{64,80... | collective-permute-start | bytes 1572872 | tf_op jit(solution)/shard_map/ppermute | solution.py:184
  36.6 9.3 %collective-permute-start.7 = (f32[5]{0:T(128)S(1)}, f32[5]{0:T(128)S(1)}, u32[]{:S(2)}, u32[]{:S(2)}) collective-permute-start(f32[5]{0:T(128)S(1)} %bitcast_multiply_fusion.f_ref), channel_id=1, source_target_pairs={{0,8},{8,0},{16,24},{24,16},{32,40},{40,32},{48,56},{56,48},{64,72... | collective-permute-start | bytes 68 | tf_op jit(solution)/shard_map/ppermute | solution.py:184
  46.8 3.8 %collective-permute-start.8 = (bf16[2,256,512]{2,1,0:T(8,128)(2,1)S(1)}, bf16[2,256,512]{2,1,0:T(8,128)(2,1)S(1)}, u32[]{:S(2)}, u32[]{:S(2)}) collective-permute-start(bf16[2,256,512]{2,1,0:T(8,128)(2,1)S(1)} %shard_map.89), channel_id=1, source_target_pairs={{0,8},{8,0},{16,24},{24,16},{32,40},{40,32},{48,56},{56,48},{64,72... | collective-permute-start | bytes 1572872 | tf_op jit(solution)/shard_map/ppermute | solution.py:184
  49.7 29.2 %copy-start.2 = (bf16[1,4,256,256]{3,2,1,0:T(8,128)(2,1)S(1)}, bf16[1,4,256,256]{3,2,1,0:T(8,128)(2,1)}, u32[]{:S(2)}) copy-start(bf16[1,4,256,256]{3,2,1,0:T(8,128)(2,1)} %param.9) | copy-start | bytes 1572868
  51.5 25.9 %collective-permute-start.12 = (bf16[2,256,768]{2,1,0:T(8,128)(2,1)S(1)}, bf16[2,256,768]{2,1,0:T(8,128)(2,1)S(1)}, u32[]{:S(2)}, u32[]{:S(2)}) collective-permute-start(bf16[2,256,768]{2,1,0:T(8,128)(2,1)S(1)} %get-tuple-element.33.own_ref), channel_id=1, source_target_pairs={{1,2},{3,4},{5,6},{2,1},{4,3},{6,5},{9,10},{11,12},{13,14},{10,9},... | collective-permute-start | bytes 2359304 | tf_op jit(solution)/shard_map/ppermute | solution.py:211
  56.5 22.3 %collective-permute-start.11 = (bf16[2,256,768]{2,1,0:T(8,128)(2,1)S(1)}, bf16[2,256,768]{2,1,0:T(8,128)(2,1)S(1)}, u32[]{:S(2)}, u32[]{:S(2)}) collective-permute-start(bf16[2,256,768]{2,1,0:T(8,128)(2,1)S(1)} %get-tuple-element.33.own_ref), channel_id=1, source_target_pairs={{0,1},{2,3},{4,5},{6,7},{1,0},{3,2},{5,4},{7,6},{8,9},{10,11},{12,... | collective-permute-start | bytes 2359304 | tf_op jit(solution)/shard_map/ppermute | solution.py:210
  58.4 20.4 %copy-start.3 = (f32[4]{0:T(128)S(1)}, f32[4]{0:T(128)}, u32[]{:S(2)}) copy-start(f32[4]{0:T(128)} %occ_ref.3) | copy-start | bytes 52
  58.5 20.4 %copy-start.4 = (s32[4]{0:T(128)S(1)}, s32[4]{0:T(128)}, u32[]{:S(2)}) copy-start(s32[4]{0:T(128)} %off_ref.3) | copy-start | bytes 52
  58.5 24.9 %collective-permute-start.10 = (bf16[2,256,256]{2,1,0:T(8,128)(2,1)S(1)}, bf16[2,256,256]{2,1,0:T(8,128)(2,1)S(1)}, u32[]{:S(2)}, u32[]{:S(2)}) collective-permute-start(bf16[2,256,256]{2,1,0:T(8,128)(2,1)S(1)} %get-tuple-element.32.own_ref), channel_id=1, source_target_pairs={{0,1},{2,3},{4,5},{6,7},{1,0},{3,2},{5,4},{7,6},{8,9},{10,11},{12,... | collective-permute-start | bytes 786440 | tf_op jit(solution)/shard_map/ppermute | solution.py:213
  62.4 20.9 %collective-permute-start.9 = (bf16[2,256,256]{2,1,0:T(8,128)(2,1)S(1)}, bf16[2,256,256]{2,1,0:T(8,128)(2,1)S(1)}, u32[]{:S(2)}, u32[]{:S(2)}) collective-permute-start(bf16[2,256,256]{2,1,0:T(8,128)(2,1)S(1)} %get-tuple-element.32.own_ref), channel_id=1, source_target_pairs={{1,2},{3,4},{5,6},{2,1},{4,3},{6,5},{9,10},{11,12},{13,14},{10,9},... | collective-permute-start | bytes 786440 | tf_op jit(solution)/shard_map/ppermute | solution.py:212

commit v5 on v3

--- a/solution.py
+++ b/solution.py
@@ -92,9 +92,9 @@
 
 
 def stage(a, b):
-    shape = jax.ShapeDtypeStruct(SHAPE, BF16)
+    shapes = [jax.ShapeDtypeStruct(v.shape, BF16) for v in (a, b)]
     return pl.pallas_call(
-        stage_kernel, out_shape=[shape, shape], in_specs=[VMEM, VMEM], out_specs=[VMEM, VMEM], compiler_params=PARAMS
+        stage_kernel, out_shape=shapes, in_specs=[VMEM, VMEM], out_specs=[VMEM, VMEM], compiler_params=PARAMS
     )(a, b)
 
 
@@ -159,14 +159,14 @@
     xl = lesser.reshape(SHAPE)
     xg = greater.reshape(SHAPE)
     mats = coupling[0]
-    xlv, xgv = stage(xl, xg)
+    xgv, mats = stage(xg, mats)
     f = weights * readers[0].astype(F32)
 
     yl = kz(xl, swap_route(count, 2))
     zg = kz(xg, plane_route(count, -1))
     cg = kz(xg, swap_route(count, 1))
     fy = kz(f, swap_route(count, 2))
-    yl, f, fy, pos, xlv, xgv = lax.optimization_barrier((yl, f, fy, pos, xlv, xgv))
+    yl, f, fy, pos, xgv, mats = lax.optimization_barrier((yl, f, fy, pos, xgv, mats))
     zl = kz(yl, plane_route(count, 1))
     czg = kz(zg, swap_route(count, 1))
     pg = combine(pair_partial_kernel, pos, fy, xgv, zg, cg, czg)
@@ -174,10 +174,10 @@
     late, _ = lax.optimization_barrier((f, pg))
     fc = kz(late, swap_route(count, 1))
     zl, fc = lax.optimization_barrier((zl, fc))
-    ql = combine(core_partial_kernel, pos, fc, xlv, yl, zl)
+    ql = combine(core_partial_kernel, pos, fc, xl, yl, zl)
     rl = kz(ql, swap_route(count, 1))
     wg = combine(greater_window_kernel, pos, f, xgv, cg, rg)
-    wl = combine(lesser_window_kernel, pos, f, xlv, yl, zl, rl)
+    wl = combine(lesser_window_kernel, pos, f, xl, yl, zl, rl)
 
     odd_pairs, even_pairs = pair_route(energies, 1), pair_route(energies, 0)
     bl = lax.ppermute(wl, "en", even_pairs)

time: 83.2 us -> 83.2 us (level)
  no operation moved by 1% of the time
where the time goes in v5:
time: 83.2 us; the launch traced here: 82.7 us
  starting transfers between devices  44.4 us (53%)
  waiting for transfers between devices  25.6 us (31%)
  Pallas kernels  9.59 us (12%)
  local copies, waits for them, and re-layouts  2.1 us (3%)
  between operations  0.87 us (1%)
    ppermute x9, starting transfers between devices, kz(): return lax.ppermute(block, 'kz', route)  30.9 us
    ppermute x9, waiting for transfers between devices, kz(): return lax.ppermute(block, 'kz', route)  11.2 us
    ppermute x1, waiting for transfers between devices, local(): al = lax.ppermute(wl, 'en', odd_pairs)  6.32 us
    pallas_call x2, Pallas kernels, sigma(): pl.pallas_call(functools.partial(sigma_kernel, plus_up=plus_up), out_shap...  6.04 us
    ppermute x1, waiting for transfers between devices, local(): ag = lax.ppermute(wg, 'en', odd_pairs)  5.74 us
    ppermute x1, starting transfers between devices, local(): al = lax.ppermute(wl, 'en', odd_pairs)  4.88 us
    ppermute x1, starting transfers between devices, local(): ag = lax.ppermute(wg, 'en', odd_pairs)  4.84 us
    pallas_call x4, Pallas kernels, combine(): pl.pallas_call(kernel, out_shape=jax.ShapeDtypeStruct(SHAPE, BF16), in_sp...  3.48 us
  transfers between devices with their start and end apart: 13, of which 8 were waited for; matrix products, arithmetic and copies ran while one was open for 0% of the time, Pallas kernels for 8%

profile of v5, /device:TPU:6, one launch (start us, length us, event | category | flops | bytes accessed | tf_op | source)
XLA Modules:
  0.0 82.7 jit_solution(8897208750293487100)
XLA Ops:
  0.6 0.0 copy-start.5
  0.6 0.0 copy-start.6
  0.6 11.5 %collective-permute-start.3 = (bf16[2,256,512]{2,1,0:T(8,128)(2,1)}, bf16[2,256,512]{2,1,0:T(8,128)(2,1)S(1)}, u32[]{:S(2)}, u32[]{:S(2)}) collective-permute-start(bf16[2,256,512]{2,1,0:T(8,128)(2,1)} %bitcast.18), channel_id=1, source_target_pairs={{0,480},{8,488},{16,48},{24,56},{32,0},{40,8},{48,80},{56,88},{64,... | collective-permute-start | bytes 1572872 | tf_op jit(solution)/shard_map/ppermute | solution.py:157
  12.2 1.9 %collective-permute-start = (bf16[2,256,512]{2,1,0:T(8,128)(2,1)}, bf16[2,256,512]{2,1,0:T(8,128)(2,1)S(1)}, u32[]{:S(2)}, u32[]{:S(2)}) collective-permute-start(bf16[2,256,512]{2,1,0:T(8,128)(2,1)} %bitcast.14), channel_id=1, source_target_pairs={{0,16},{8,24},{16,0},{24,8},{32,48},{40,56},{48,32},{56,40},{64,80... | collective-permute-start | bytes 1572872 | tf_op jit(solution)/shard_map/ppermute | solution.py:157
  14.1 1.9 %collective-permute-start.4 = (bf16[2,256,512]{2,1,0:T(8,128)(2,1)}, bf16[2,256,512]{2,1,0:T(8,128)(2,1)S(1)}, u32[]{:S(2)}, u32[]{:S(2)}) collective-permute-start(bf16[2,256,512]{2,1,0:T(8,128)(2,1)} %bitcast.19), channel_id=1, source_target_pairs={{0,8},{8,0},{16,24},{24,16},{32,40},{40,32},{48,56},{56,48},{64,72... | collective-permute-start | bytes 1572872 | tf_op jit(solution)/shard_map/ppermute | solution.py:157
  16.1 0.0 copy-done.5
  16.1 0.0 copy-done.6
  16.1 3.9 %collective-permute-start.1 = (f32[5]{0:T(128)S(1)}, f32[5]{0:T(128)S(1)}, u32[]{:S(2)}, u32[]{:S(2)}) collective-permute-start(f32[5]{0:T(128)S(1)} %bitcast_multiply_fusion.f_ref), channel_id=1, source_target_pairs={{0,16},{8,24},{16,0},{24,8},{32,48},{40,56},{48,32},{56,40},{64,80... | collective-permute-start | bytes 68 | tf_op jit(solution)/shard_map/ppermute | solution.py:157
  20.0 0.0 copy-start.1
  20.0 1.0 %copy-done.1 = bf16[1,4,256,256]{3,2,1,0:T(8,128)(2,1)S(1)} copy-done((bf16[1,4,256,256]{3,2,1,0:T(8,128)(2,1)S(1)}, bf16[1,4,256,256]{3,2,1,0:T(8,128)(2,1)}, u32[]{:S(2)}) %copy-start.1) | copy-done | bytes 524312
  21.1 0.0 copy-start.2
  21.1 1.0 %copy-done.2 = bf16[1,2,1,256,512]{4,3,2,1,0:T(8,128)(2,1)S(1)} copy-done((bf16[1,2,1,256,512]{4,3,2,1,0:T(8,128)(2,1)S(1)}, bf16[1,2,1,256,512]{4,3,2,1,0:T(8,128)(2,1)}, u32[]{:S(2)}) %copy-start.2) | copy-done | bytes 524312
  22.1 0.1 shard_map.86
  22.2 1.5 %collective-permute-done.3.z_ref = bf16[2,256,512]{2,1,0:T(8,128)(2,1)S(1)} collective-permute-done((bf16[2,256,512]{2,1,0:T(8,128)(2,1)}, bf16[2,256,512]{2,1,0:T(8,128)(2,1)S(1)}, u32[]{:S(2)}, u32[]{:S(2)}) %collective-permute-start.3) | collective-permute-done | bytes 524320 | tf_op jit(solution)/shard_map/ppermute | solution.py:157
  23.7 1.9 %collective-permute-start.5 = (bf16[2,256,512]{2,1,0:T(8,128)(2,1)S(1)}, bf16[2,256,512]{2,1,0:T(8,128)(2,1)S(1)}, u32[]{:S(2)}, u32[]{:S(2)}) collective-permute-start(bf16[2,256,512]{2,1,0:T(8,128)(2,1)S(1)} %collective-permute-done.3.z_ref), channel_id=1, source_target_pairs={{0,8},{8,0},{16,24},{24,16},{32,40},{40,32},{48,56},{56,48},{64,72... | collective-permute-start | bytes 1572872 | tf_op jit(solution)/shard_map/ppermute | solution.py:157
  25.6 0.1 pad_add_fusion.pos_ref
  25.7 2.1 %collective-permute-done.1.f_ref = f32[5]{0:T(128)S(1)} collective-permute-done((f32[5]{0:T(128)S(1)}, f32[5]{0:T(128)S(1)}, u32[]{:S(2)}, u32[]{:S(2)}) %collective-permute-start.1) | collective-permute-done | bytes 52 | tf_op jit(solution)/shard_map/ppermute | solution.py:157
  27.8 0.0 collective-permute-done.y_ref
  27.8 0.0 copy-start
  27.8 2.0 %collective-permute-start.2 = (bf16[2,256,512]{2,1,0:T(8,128)(2,1)S(1)}, bf16[2,256,512]{2,1,0:T(8,128)(2,1)S(1)}, u32[]{:S(2)}, u32[]{:S(2)}) collective-permute-start(bf16[2,256,512]{2,1,0:T(8,128)(2,1)S(1)} %collective-permute-done.y_ref), channel_id=1, source_target_pairs={{0,32},{8,40},{16,496},{24,504},{32,64},{40,72},{48,16},{56,24},{6... | collective-permute-start | bytes 1572872 | tf_op jit(solution)/shard_map/ppermute | solution.py:157
  29.8 0.0 collective-permute-done.4.c_ref
  29.8 0.0 collective-permute-done.5.cz_ref
  29.8 0.9 %shard_map.87 = bf16[2,256,512]{2,1,0:T(8,128)(2,1)S(1)} custom-call(s32[3]{0:T(128)S(1)} %pad_add_fusion.pos_ref, f32[5]{0:T(128)S(1)} %collective-permute-done.1.f_ref, bf16[2,256,512]{2,1,0:T(8,128)(2,1)S(1)} %get-tuple-element.19.x_ref, bf16[2,256,512]{2,1,0:T(8,128)(2,1)S(1)} %collective-permute-done.3.z_ref, ...), custom_call_target="tpu_custom_call" | custom-call | flops 2097152 | bytes 2097152 | tf_op jit(solution)/shard_map/pallas_call | solution.py:79
  30.8 3.8 %collective-permute-start.10 = (bf16[2,256,512]{2,1,0:T(8,128)(2,1)S(1)}, bf16[2,256,512]{2,1,0:T(8,128)(2,1)S(1)}, u32[]{:S(2)}, u32[]{:S(2)}) collective-permute-start(bf16[2,256,512]{2,1,0:T(8,128)(2,1)S(1)} %shard_map.87), channel_id=1, source_target_pairs={{0,16},{8,24},{16,0},{24,8},{32,48},{40,56},{48,32},{56,40},{64,80... | collective-permute-start | bytes 1572872 | tf_op jit(solution)/shard_map/ppermute | solution.py:157
  34.6 1.9 %collective-permute-start.6 = (f32[5]{0:T(128)S(1)}, f32[5]{0:T(128)S(1)}, u32[]{:S(2)}, u32[]{:S(2)}) collective-permute-start(f32[5]{0:T(128)S(1)} %bitcast_multiply_fusion.f_ref), channel_id=1, source_target_pairs={{0,8},{8,0},{16,24},{24,16},{32,40},{40,32},{48,56},{56,48},{64,72... | collective-permute-start | bytes 68 | tf_op jit(solution)/shard_map/ppermute | solution.py:157
  36.5 7.4 %collective-permute-done.2.z_ref = bf16[2,256,512]{2,1,0:T(8,128)(2,1)S(1)} collective-permute-done((bf16[2,256,512]{2,1,0:T(8,128)(2,1)S(1)}, bf16[2,256,512]{2,1,0:T(8,128)(2,1)S(1)}, u32[]{:S(2)}, u32[]{:S(2)}) %collective-permute-start.2) | collective-permute-done | bytes 524320 | tf_op jit(solution)/shard_map/ppermute | solution.py:157
  43.9 0.0 collective-permute-done.6.f_ref
  43.9 0.0 copy-done
  43.9 0.8 %shard_map.88 = bf16[2,256,512]{2,1,0:T(8,128)(2,1)S(1)} custom-call(s32[3]{0:T(128)S(1)} %pad_add_fusion.pos_ref, f32[5]{0:T(128)S(1)} %collective-permute-done.6.f_ref, bf16[2,256,512]{2,1,0:T(8,128)(2,1)S(1)} %bitcast.15, bf16[2,256,512]{2,1,0:T(8,128)(2,1)S(1)} %collective-permute-done.y_ref, bf16[2,256,512]{2,1,0:T(8,128)(2,1)S(1)} %collective-permute-done.2.z_ref), custom_call_target="tpu_custom_call" | custom-call | flops 2097152 | bytes 2097152 | tf_op jit(solution)/shard_map/pallas_call | solution.py:79
  44.7 1.9 %collective-permute-start.7 = (bf16[2,256,512]{2,1,0:T(8,128)(2,1)S(1)}, bf16[2,256,512]{2,1,0:T(8,128)(2,1)S(1)}, u32[]{:S(2)}, u32[]{:S(2)}) collective-permute-start(bf16[2,256,512]{2,1,0:T(8,128)(2,1)S(1)} %shard_map.88), channel_id=1, source_target_pairs={{0,8},{8,0},{16,24},{24,16},{32,40},{40,32},{48,56},{56,48},{64,72... | collective-permute-start | bytes 1572872 | tf_op jit(solution)/shard_map/ppermute | solution.py:157
  46.7 0.2 collective-permute-done.10.r_ref
  46.9 0.8 shard_map.91.own_ref
  47.7 0.0 copy-start.3
  47.7 0.0 copy-start.4
  47.7 4.8 %collective-permute-start.12 = (bf16[2,256,512]{2,1,0:T(8,128)(2,1)S(1)}, bf16[2,256,512]{2,1,0:T(8,128)(2,1)S(1)}, u32[]{:S(2)}, u32[]{:S(2)}) collective-permute-start(bf16[2,256,512]{2,1,0:T(8,128)(2,1)S(1)} %shard_map.91.own_ref), channel_id=1, source_target_pairs={{1,2},{3,4},{5,6},{2,1},{4,3},{6,5},{9,10},{11,12},{13,14},{10,9},... | collective-permute-start | bytes 1572872 | tf_op jit(solution)/shard_map/ppermute | solution.py:186
  52.5 1.9 %collective-permute-start.11 = (bf16[2,256,512]{2,1,0:T(8,128)(2,1)S(1)}, bf16[2,256,512]{2,1,0:T(8,128)(2,1)S(1)}, u32[]{:S(2)}, u32[]{:S(2)}) collective-permute-start(bf16[2,256,512]{2,1,0:T(8,128)(2,1)S(1)} %shard_map.91.own_ref), channel_id=1, source_target_pairs={{0,1},{2,3},{4,5},{6,7},{1,0},{3,2},{5,4},{7,6},{8,9},{10,11},{12,... | collective-permute-start | bytes 1572872 | tf_op jit(solution)/shard_map/ppermute | solution.py:185
  54.5 0.0 collective-permute-done.7.r_ref
  54.5 0.9 %shard_map.89.own_ref = bf16[2,256,512]{2,1,0:T(8,128)(2,1)S(1)} custom-call(s32[3]{0:T(128)S(1)} %pad_add_fusion.pos_ref, f32[5]{0:T(128)S(1)} %bitcast_multiply_fusion.f_ref, bf16[2,256,512]{2,1,0:T(8,128)(2,1)S(1)} %bitcast.16, bf16[2,256,512]{2,1,0:T(8,128)(2,1)S(1)} %collective-permute-done.y_ref, ...), custom_call_target="tpu_custom_call" | custom-call | flops 2097152 | bytes 2097152 | tf_op jit(solution)/shard_map/pallas_call | solution.py:79
  55.4 4.9 %collective-permute-start.9 = (bf16[2,256,512]{2,1,0:T(8,128)(2,1)S(1)}, bf16[2,256,512]{2,1,0:T(8,128)(2,1)S(1)}, u32[]{:S(2)}, u32[]{:S(2)}) collective-permute-start(bf16[2,256,512]{2,1,0:T(8,128)(2,1)S(1)} %shard_map.89.own_ref), channel_id=1, source_target_pairs={{1,2},{3,4},{5,6},{2,1},{4,3},{6,5},{9,10},{11,12},{13,14},{10,9},... | collective-permute-start | bytes 1572872 | tf_op jit(solution)/shard_map/ppermute | solution.py:184
  60.3 1.9 %collective-permute-start.8 = (bf16[2,256,512]{2,1,0:T(8,128)(2,1)S(1)}, bf16[2,256,512]{2,1,0:T(8,128)(2,1)S(1)}, u32[]{:S(2)}, u32[]{:S(2)}) collective-permute-start(bf16[2,256,512]{2,1,0:T(8,128)(2,1)S(1)} %shard_map.89.own_ref), channel_id=1, source_target_pairs={{0,1},{2,3},{4,5},{6,7},{1,0},{3,2},{5,4},{7,6},{8,9},{10,11},{12,... | collective-permute-start | bytes 1572872 | tf_op jit(solution)/shard_map/ppermute | solution.py:183
  62.2 5.7 %collective-permute-done.12.a_ref = bf16[2,256,512]{2,1,0:T(8,128)(2,1)S(1)} collective-permute-done((bf16[2,256,512]{2,1,0:T(8,128)(2,1)S(1)}, bf16[2,256,512]{2,1,0:T(8,128)(2,1)S(1)}, u32[]{:S(2)}, u32[]{:S(2)}) %collective-permute-start.12) | collective-permute-done | bytes 524320 | tf_op jit(solution)/shard_map/ppermute | solution.py:186
  67.9 1.2 %collective-permute-done.11.b_ref = bf16[2,256,512]{2,1,0:T(8,128)(2,1)S(1)} collective-permute-done((bf16[2,256,512]{2,1,0:T(8,128)(2,1)S(1)}, bf16[2,256,512]{2,1,0:T(8,128)(2,1)S(1)}, u32[]{:S(2)}, u32[]{:S(2)}) %collective-permute-start.11) | collective-permute-done | bytes 524320 | tf_op jit(solution)/shard_map/ppermute | solution.py:185
  69.2 0.0 copy-done.3
  69.2 0.0 copy-done.4
  69.2 3.1 %shard_map.92 = bf16[2,256,512]{2,1,0:T(8,128)(2,1)} custom-call(s32[3]{0:T(128)S(1)} %pad_add_fusion.pos_ref, f32[4]{0:T(128)S(1)} %copy-done.3, s32[4]{0:T(128)S(1)} %copy-done.4, bf16[2,256,512]{2,1,0:T(8,128)(2,1)S(1)} %shard_map.91.own_ref, bf16[2,256,512]{2,1,0:T(8,128)(2,1)S(1)} %collective-permute-done.11.b_ref, ...), custom_call_target="tpu_custom_call" | custom-call | flops 1073741824 | bytes 3145728 | tf_op jit(solution)/shard_map/pallas_call | solution.py:140
  72.3 6.3 %collective-permute-done.9.a_ref = bf16[2,256,512]{2,1,0:T(8,128)(2,1)S(1)} collective-permute-done((bf16[2,256,512]{2,1,0:T(8,128)(2,1)S(1)}, bf16[2,256,512]{2,1,0:T(8,128)(2,1)S(1)}, u32[]{:S(2)}, u32[]{:S(2)}) %collective-permute-start.9) | collective-permute-done | bytes 524320 | tf_op jit(solution)/shard_map/ppermute | solution.py:184
  78.6 1.1 %collective-permute-done.8.b_ref = bf16[2,256,512]{2,1,0:T(8,128)(2,1)S(1)} collective-permute-done((bf16[2,256,512]{2,1,0:T(8,128)(2,1)S(1)}, bf16[2,256,512]{2,1,0:T(8,128)(2,1)S(1)}, u32[]{:S(2)}, u32[]{:S(2)}) %collective-permute-start.8) | collective-permute-done | bytes 524320 | tf_op jit(solution)/shard_map/ppermute | solution.py:183
  79.7 3.0 %shard_map.90 = bf16[2,256,512]{2,1,0:T(8,128)(2,1)} custom-call(s32[3]{0:T(128)S(1)} %pad_add_fusion.pos_ref, f32[4]{0:T(128)S(1)} %copy-done.3, s32[4]{0:T(128)S(1)} %copy-done.4, bf16[2,256,512]{2,1,0:T(8,128)(2,1)S(1)} %shard_map.89.own_ref, bf16[2,256,512]{2,1,0:T(8,128)(2,1)S(1)} %collective-permute-done.8.b_ref, ...), custom_call_target="tpu_custom_call" | custom-call | flops 1073741824 | bytes 3145728 | tf_op jit(solution)/shard_map/pallas_call | solution.py:140
  (1 shorter events, 0.0 us)
Async XLA Ops:
  0.6 15.4 %copy-start.5 = (f32[5]{0:T(128)S(1)}, f32[5]{0:T(128)}, u32[]{:S(2)}) copy-start(f32[5]{0:T(128)} %param.13) | copy-start | bytes 64
  0.6 15.4 %copy-start.6 = (s32[1,5]{1,0:T(1,128)S(1)}, s32[1,5]{1,0:T(1,128)}, u32[]{:S(2)}) copy-start(s32[1,5]{1,0:T(1,128)} %param.12) | copy-start | bytes 64
  0.6 23.0 %collective-permute-start.3 = (bf16[2,256,512]{2,1,0:T(8,128)(2,1)}, bf16[2,256,512]{2,1,0:T(8,128)(2,1)S(1)}, u32[]{:S(2)}, u32[]{:S(2)}) collective-permute-start(bf16[2,256,512]{2,1,0:T(8,128)(2,1)} %bitcast.18), channel_id=1, source_target_pairs={{0,480},{8,488},{16,48},{24,56},{32,0},{40,8},{48,80},{56,88},{64,... | collective-permute-start | bytes 1572872 | tf_op jit(solution)/shard_map/ppermute | solution.py:157
  12.2 15.6 %collective-permute-start = (bf16[2,256,512]{2,1,0:T(8,128)(2,1)}, bf16[2,256,512]{2,1,0:T(8,128)(2,1)S(1)}, u32[]{:S(2)}, u32[]{:S(2)}) collective-permute-start(bf16[2,256,512]{2,1,0:T(8,128)(2,1)} %bitcast.14), channel_id=1, source_target_pairs={{0,16},{8,24},{16,0},{24,8},{32,48},{40,56},{48,32},{56,40},{64,80... | collective-permute-start | bytes 1572872 | tf_op jit(solution)/shard_map/ppermute | solution.py:157
  14.1 15.7 %collective-permute-start.4 = (bf16[2,256,512]{2,1,0:T(8,128)(2,1)}, bf16[2,256,512]{2,1,0:T(8,128)(2,1)S(1)}, u32[]{:S(2)}, u32[]{:S(2)}) collective-permute-start(bf16[2,256,512]{2,1,0:T(8,128)(2,1)} %bitcast.19), channel_id=1, source_target_pairs={{0,8},{8,0},{16,24},{24,16},{32,40},{40,32},{48,56},{56,48},{64,72... | collective-permute-start | bytes 1572872 | tf_op jit(solution)/shard_map/ppermute | solution.py:157
  16.1 11.7 %collective-permute-start.1 = (f32[5]{0:T(128)S(1)}, f32[5]{0:T(128)S(1)}, u32[]{:S(2)}, u32[]{:S(2)}) collective-permute-start(f32[5]{0:T(128)S(1)} %bitcast_multiply_fusion.f_ref), channel_id=1, source_target_pairs={{0,16},{8,24},{16,0},{24,8},{32,48},{40,56},{48,32},{56,40},{64,80... | collective-permute-start | bytes 68 | tf_op jit(solution)/shard_map/ppermute | solution.py:157
  20.0 1.0 %copy-start.1 = (bf16[1,4,256,256]{3,2,1,0:T(8,128)(2,1)S(1)}, bf16[1,4,256,256]{3,2,1,0:T(8,128)(2,1)}, u32[]{:S(2)}) copy-start(bf16[1,4,256,256]{3,2,1,0:T(8,128)(2,1)} %param.9) | copy-start | bytes 1572868
  21.1 1.0 %copy-start.2 = (bf16[1,2,1,256,512]{4,3,2,1,0:T(8,128)(2,1)S(1)}, bf16[1,2,1,256,512]{4,3,2,1,0:T(8,128)(2,1)}, u32[]{:S(2)}) copy-start(bf16[1,2,1,256,512]{4,3,2,1,0:T(8,128)(2,1)} %param.8) | copy-start | bytes 1572868
  23.7 6.1 %collective-permute-start.5 = (bf16[2,256,512]{2,1,0:T(8,128)(2,1)S(1)}, bf16[2,256,512]{2,1,0:T(8,128)(2,1)S(1)}, u32[]{:S(2)}, u32[]{:S(2)}) collective-permute-start(bf16[2,256,512]{2,1,0:T(8,128)(2,1)S(1)} %collective-permute-done.3.z_ref), channel_id=1, source_target_pairs={{0,8},{8,0},{16,24},{24,16},{32,40},{40,32},{48,56},{56,48},{64,72... | collective-permute-start | bytes 1572872 | tf_op jit(solution)/shard_map/ppermute | solution.py:157
  27.8 16.1 %copy-start = (bf16[1,2,1,256,512]{4,3,2,1,0:T(8,128)(2,1)S(1)}, bf16[1,2,1,256,512]{4,3,2,1,0:T(8,128)(2,1)}, u32[]{:S(2)}) copy-start(bf16[1,2,1,256,512]{4,3,2,1,0:T(8,128)(2,1)} %param.7) | copy-start | bytes 1572868
  27.8 16.1 %collective-permute-start.2 = (bf16[2,256,512]{2,1,0:T(8,128)(2,1)S(1)}, bf16[2,256,512]{2,1,0:T(8,128)(2,1)S(1)}, u32[]{:S(2)}, u32[]{:S(2)}) collective-permute-start(bf16[2,256,512]{2,1,0:T(8,128)(2,1)S(1)} %collective-permute-done.y_ref), channel_id=1, source_target_pairs={{0,32},{8,40},{16,496},{24,504},{32,64},{40,72},{48,16},{56,24},{6... | collective-permute-start | bytes 1572872 | tf_op jit(solution)/shard_map/ppermute | solution.py:157
  30.8 16.1 %collective-permute-start.10 = (bf16[2,256,512]{2,1,0:T(8,128)(2,1)S(1)}, bf16[2,256,512]{2,1,0:T(8,128)(2,1)S(1)}, u32[]{:S(2)}, u32[]{:S(2)}) collective-permute-start(bf16[2,256,512]{2,1,0:T(8,128)(2,1)S(1)} %shard_map.87), channel_id=1, source_target_pairs={{0,16},{8,24},{16,0},{24,8},{32,48},{40,56},{48,32},{56,40},{64,80... | collective-permute-start | bytes 1572872 | tf_op jit(solution)/shard_map/ppermute | solution.py:157
  34.6 9.3 %collective-permute-start.6 = (f32[5]{0:T(128)S(1)}, f32[5]{0:T(128)S(1)}, u32[]{:S(2)}, u32[]{:S(2)}) collective-permute-start(f32[5]{0:T(128)S(1)} %bitcast_multiply_fusion.f_ref), channel_id=1, source_target_pairs={{0,8},{8,0},{16,24},{24,16},{32,40},{40,32},{48,56},{56,48},{64,72... | collective-permute-start | bytes 68 | tf_op jit(solution)/shard_map/ppermute | solution.py:157
  44.7 9.7 %collective-permute-start.7 = (bf16[2,256,512]{2,1,0:T(8,128)(2,1)S(1)}, bf16[2,256,512]{2,1,0:T(8,128)(2,1)S(1)}, u32[]{:S(2)}, u32[]{:S(2)}) collective-permute-start(bf16[2,256,512]{2,1,0:T(8,128)(2,1)S(1)} %shard_map.88), channel_id=1, source_target_pairs={{0,8},{8,0},{16,24},{24,16},{32,40},{40,32},{48,56},{56,48},{64,72... | collective-permute-start | bytes 1572872 | tf_op jit(solution)/shard_map/ppermute | solution.py:157
  47.7 21.5 %copy-start.3 = (f32[4]{0:T(128)S(1)}, f32[4]{0:T(128)}, u32[]{:S(2)}) copy-start(f32[4]{0:T(128)} %occ_ref.3) | copy-start | bytes 52
  47.7 21.5 %copy-start.4 = (s32[4]{0:T(128)S(1)}, s32[4]{0:T(128)}, u32[]{:S(2)}) copy-start(s32[4]{0:T(128)} %off_ref.3) | copy-start | bytes 52
  47.7 20.3 %collective-permute-start.12 = (bf16[2,256,512]{2,1,0:T(8,128)(2,1)S(1)}, bf16[2,256,512]{2,1,0:T(8,128)(2,1)S(1)}, u32[]{:S(2)}, u32[]{:S(2)}) collective-permute-start(bf16[2,256,512]{2,1,0:T(8,128)(2,1)S(1)} %shard_map.91.own_ref), channel_id=1, source_target_pairs={{1,2},{3,4},{5,6},{2,1},{4,3},{6,5},{9,10},{11,12},{13,14},{10,9},... | collective-permute-start | bytes 1572872 | tf_op jit(solution)/shard_map/ppermute | solution.py:186
  52.5 16.7 %collective-permute-start.11 = (bf16[2,256,512]{2,1,0:T(8,128)(2,1)S(1)}, bf16[2,256,512]{2,1,0:T(8,128)(2,1)S(1)}, u32[]{:S(2)}, u32[]{:S(2)}) collective-permute-start(bf16[2,256,512]{2,1,0:T(8,128)(2,1)S(1)} %shard_map.91.own_ref), channel_id=1, source_target_pairs={{0,1},{2,3},{4,5},{6,7},{1,0},{3,2},{5,4},{7,6},{8,9},{10,11},{12,... | collective-permute-start | bytes 1572872 | tf_op jit(solution)/shard_map/ppermute | solution.py:185
  55.4 23.2 %collective-permute-start.9 = (bf16[2,256,512]{2,1,0:T(8,128)(2,1)S(1)}, bf16[2,256,512]{2,1,0:T(8,128)(2,1)S(1)}, u32[]{:S(2)}, u32[]{:S(2)}) collective-permute-start(bf16[2,256,512]{2,1,0:T(8,128)(2,1)S(1)} %shard_map.89.own_ref), channel_id=1, source_target_pairs={{1,2},{3,4},{5,6},{2,1},{4,3},{6,5},{9,10},{11,12},{13,14},{10,9},... | collective-permute-start | bytes 1572872 | tf_op jit(solution)/shard_map/ppermute | solution.py:184
  60.3 19.4 %collective-permute-start.8 = (bf16[2,256,512]{2,1,0:T(8,128)(2,1)S(1)}, bf16[2,256,512]{2,1,0:T(8,128)(2,1)S(1)}, u32[]{:S(2)}, u32[]{:S(2)}) collective-permute-start(bf16[2,256,512]{2,1,0:T(8,128)(2,1)S(1)} %shard_map.89.own_ref), channel_id=1, source_target_pairs={{0,1},{2,3},{4,5},{6,7},{1,0},{3,2},{5,4},{7,6},{8,9},{10,11},{12,... | collective-permute-start | bytes 1572872 | tf_op jit(solution)/shard_map/ppermute | solution.py:183
